TPU v7x, 32 devices: a whole 2x2x4 slice. The times are simulated.
32 devices in a mesh: row: 4 (over y, core), col: 8 (over z, x).
Axes of the slice: x: 2, y: 2, z: 4, core: 2. Of those that a mesh axis runs over, the one named last changes fastest.
Arguments:
- user_emb: float32 [4, 8, 2048, 128], P('row', 'col'), may hold values from -2.4 to 2.4
- item_emb: float32 [8, 4, 1024, 128], P('col', 'row'), may hold values from -2.4 to 2.4
- tile_vals: bfloat16 [4, 8, 512, 128, 128], P('row', 'col'), may hold values from 0 to 0.029907227
- tile_rows: int32 [4, 8, 512], P('row', 'col'), may hold values from 0 to 127
- tile_cols: int32 [4, 8, 512], P('row', 'col'), may hold values from 0 to 31
- tile_count: int32 [4, 8], P('row', 'col'), may hold values from 128 to 512, as said below
- pair_users: int32 [16384], P(('row', 'col')), may hold values from 0 to 65535, as said below
- pair_items: int32 [16384], P(('row', 'col')), may hold values from 0 to 32767, as said below
- negatives: int32 [1024], replicated, may hold values from 0 to 32767, as said below
Outputs:
- user_final: float32 [4, 8, 2048, 128], P('row', 'col')
- item_final: float32 [8, 4, 1024, 128], P('col', 'row')
- bpr_terms: float32 [16384, 1024], P(('row', 'col'))
Inputs may be any that keep to these rules, and one draw needn't show every extreme that they name: `pair_users`: taken in aligned blocks of 512 entries, at most 32 entries of one block name users that one device holds in user_emb; in every draw some device's users are named exactly 32 times in every block. `pair_items`: taken in aligned blocks of 512 entries, at most 32 entries of one block name items that one device holds in item_emb; in every draw some device's items are named exactly 32 times in every block. `tile_count`: some block has all 512 slots live. `negatives`: entry j names an item that the device with row index (j // 32) // 8 and col index (j // 32) % 8 holds in item_emb.
All inputs are finite; a program needn't handle non-finite values.
Results may differ from a plain program's by a relative error of at most 0.009.
Values may be sent and summed in bfloat16 or wider, within the bound.
No kernel may reach another device: no remote copies, remote signals or barrier semaphores. Data moves between devices by JAX's collectives and lax.ppermute only.
A program may use at most 128 MiB of HBM per device.

v0:
```python
import math

import jax
import jax.numpy as jnp
from jax import lax
from jax.sharding import PartitionSpec as P


def tile_products(values_all, row_all, col_all, number, user_tiles, item_tiles):
    total = values_all.shape[0]
    width = math.gcd(total, 64)
    blocks = (number + width - 1) // width

    def advance(block_index, totals):
        user_part, item_part = totals
        offset = block_index * width
        values = lax.dynamic_slice_in_dim(values_all, offset, width, 0)
        row_ids = lax.dynamic_slice_in_dim(row_all, offset, width, 0)
        col_ids = lax.dynamic_slice_in_dim(col_all, offset, width, 0)
        live_mask = (offset + jnp.arange(width, dtype=jnp.int32) < number).astype(jnp.float32)[
            :, None, None
        ]
        to_users = (
            jnp.einsum(
                "tij,tje->tie", values, item_tiles[col_ids], preferred_element_type=jnp.float32
            )
            * live_mask
        )
        to_items = (
            jnp.einsum(
                "tij,tie->tje", values, user_tiles[row_ids], preferred_element_type=jnp.float32
            )
            * live_mask
        )
        return (user_part.at[row_ids].add(to_users), item_part.at[col_ids].add(to_items))

    start = (jnp.zeros(user_tiles.shape, jnp.float32), jnp.zeros(item_tiles.shape, jnp.float32))
    return lax.fori_loop(0, blocks, advance, start)


def place_requests(owner, local, devices, slots_per):
    hits = (owner[:, None] == jnp.arange(devices, dtype=jnp.int32)[None, :]).astype(jnp.int32)
    rank = jnp.sum((jnp.cumsum(hits, axis=0) - 1) * hits, axis=1)
    slot = owner * slots_per + rank
    request = jnp.zeros((devices * slots_per,), jnp.int32).at[slot].set(local)
    return (slot, request.reshape(devices, slots_per))


def on_device(
    user_emb,
    item_emb,
    tile_vals,
    tile_rows,
    tile_cols,
    tile_count,
    pair_users,
    pair_items,
    negatives,
):
    row_count = lax.axis_size("row")
    col_count = lax.axis_size("col")
    user_dev = user_emb.shape[2]
    item_dev = item_emb.shape[2]
    embed = user_emb.shape[3]
    tile_side = tile_vals.shape[-1]
    user_whole = lax.all_gather(user_emb.astype(jnp.bfloat16), "col", axis=1, tiled=True)
    item_whole = lax.all_gather(item_emb.astype(jnp.bfloat16), "row", axis=1, tiled=True)
    user_tiles = user_whole.reshape(-1, tile_side, embed)
    item_tiles = item_whole.reshape(-1, tile_side, embed)
    user_part, item_part = tile_products(
        tile_vals[0, 0], tile_rows[0, 0], tile_cols[0, 0], tile_count[0, 0], user_tiles, item_tiles
    )
    user_prop = lax.psum_scatter(
        user_part.reshape(-1, embed).astype(jnp.bfloat16), "col", scatter_dimension=0, tiled=True
    ).astype(jnp.float32)
    item_prop = lax.psum_scatter(
        item_part.reshape(-1, embed).astype(jnp.bfloat16), "row", scatter_dimension=0, tiled=True
    ).astype(jnp.float32)
    user_final = (user_emb[0, 0] + user_prop) * 0.5
    item_final = (item_emb[0, 0] + item_prop) * 0.5
    devices = row_count * col_count
    slots_per = 2 * pair_users.shape[0] // devices
    user_owner = pair_users // user_dev
    user_local = pair_users % user_dev
    item_holder = pair_items // item_dev
    item_owner = item_holder % row_count * col_count + item_holder // row_count
    item_local = pair_items % item_dev
    user_slot, user_request = place_requests(user_owner, user_local, devices, slots_per)
    item_slot, item_request = place_requests(item_owner, item_local, devices, slots_per)
    user_wanted = lax.all_to_all(
        user_request, ("row", "col"), split_axis=0, concat_axis=0, tiled=True
    )
    item_wanted = lax.all_to_all(
        item_request, ("row", "col"), split_axis=0, concat_axis=0, tiled=True
    )
    user_rows = lax.all_to_all(
        user_final[user_wanted].astype(jnp.bfloat16),
        ("row", "col"),
        split_axis=0,
        concat_axis=0,
        tiled=True,
    ).astype(jnp.float32)
    item_rows = lax.all_to_all(
        item_final[item_wanted].astype(jnp.bfloat16),
        ("row", "col"),
        split_axis=0,
        concat_axis=0,
        tiled=True,
    ).astype(jnp.float32)
    user_vec = user_rows.reshape(-1, embed)[user_slot]
    item_vec = item_rows.reshape(-1, embed)[item_slot]
    offset = (lax.axis_index("col") * row_count + lax.axis_index("row")) * item_dev
    neg_each = negatives.shape[0] // devices
    device_rank = lax.axis_index("row") * col_count + lax.axis_index("col")
    mine = lax.dynamic_slice_in_dim(negatives, device_rank * neg_each, neg_each, 0) - offset
    negative_vec = lax.all_gather(item_final[mine], ("row", "col"), axis=0, tiled=True)
    positive = jnp.sum(user_vec * item_vec, axis=1)
    against = jnp.dot(user_vec, negative_vec.T, precision=lax.Precision.HIGHEST)
    bpr_terms = jnp.log1p(jnp.exp(against - positive[:, None]))
    return (user_final.reshape(user_emb.shape), item_final.reshape(item_emb.shape), bpr_terms)


def solution(mesh):
    placed = (
        P("row", "col", None, None),
        P("col", "row", None, None),
        P("row", "col", None, None, None),
        P("row", "col", None),
        P("row", "col", None),
        P("row", "col"),
        P(("row", "col")),
        P(("row", "col")),
        P(),
    )
    return jax.shard_map(
        on_device,
        mesh=mesh,
        in_specs=placed,
        out_specs=(
            P("row", "col", None, None),
            P("col", "row", None, None),
            P(("row", "col"), None),
        ),
        check_vma=False,
    )
```

profile of v0, /device:TPU:0, one launch (start us, length us, event | category | flops | bytes accessed | tf_op | source)
XLA Modules:
  0.0 652.1 jit_solution(9102397335324973984)
XLA Ops:
  11.9 17.7 %all-gather.4.cloned.1.call-done = bf16[1,4,1024,128]{3,2,0,1:T(8,128)(2,1)} async-done(((bf16[1,1,1024,128]{3,2,0,1:T(8,128)(2,1)}), bf16[1,4,1024,128]{3,2,0,1:T(8,128)(2,1)}) %all-gather.4.cloned.1.call-update) | async-done | bytes 1048592 | tf_op jit(solution)/shard_map/all_gather | solution.py:67
  29.6 76.1 %all-gather.6.cloned.1.call-done = bf16[1,8,2048,128]{3,2,0,1:T(8,128)(2,1)} async-done(((bf16[1,1,2048,128]{3,2,0,1:T(8,128)(2,1)}), bf16[1,8,2048,128]{3,2,0,1:T(8,128)(2,1)}) %all-gather.6.cloned.1.call-update) | async-done | bytes 4194320 | tf_op jit(solution)/shard_map/all_gather | solution.py:66
  111.2 161.8 %while.12 = (s32[]{:T(128)}, f32[128,128,128]{2,1,0:T(8,128)}, f32[32,128,128]{2,1,0:T(8,128)S(1)}, s32[]{:T(128)}, s32[512]{0:T(512)}, /*index=5*/bf16[512,128,...) while((s32[]{:T(128)}, f32[128,128,128]{2,1,0:T(8,128)}, ...), condition=%wide.region_3.4_spmd, body=%wide.region_0.3_spmd.sunk | while | flops 541067840 | bytes 50343368 | solution.py:38
  114.8 4.9 convolution_multiply_fusion.4
  119.7 13.7 %scatter_fusion = f32[128,128,128]{2,1,0:T(8,128)} fusion(f32[128,128,128]{2,1,0:T(8,128)} %get-tuple-element.166, s32[64]{0:T(128)S(1)} %get-tuple-element.149, f32[64,128,128]{2,1,0:T(8,128)} %convolution_multiply_fusion.4), kind=kCustom, calls=%fused_computation.8.clone.1 | custom fusion | flops 1048576 | bytes 12583168 | tf_op jit(solution)/shard_map/while/body/scatter-add | solution.py:35
  137.7 5.2 convolution_multiply_fusion.5
  142.9 8.8 %scatter_fusion.1 = f32[32,128,128]{2,1,0:T(8,128)S(1)} fusion(f32[32,128,128]{2,1,0:T(8,128)S(1)} %get-tuple-element.167, s32[64]{0:T(128)S(1)} %get-tuple-element.150, f32[64,128,128]{2,1,0:T(8,128)} %convolution_multiply_fusion.5), kind=kCustom, calls=%fused_computation.9.clone.1 | custom fusion | flops 1048576 | bytes 12583168 | tf_op jit(solution)/shard_map/while/body/scatter-add | solution.py:35
  155.3 4.9 convolution_multiply_fusion.4
  160.2 13.6 %scatter_fusion = f32[128,128,128]{2,1,0:T(8,128)} fusion(f32[128,128,128]{2,1,0:T(8,128)} %get-tuple-element.166, s32[64]{0:T(128)S(1)} %get-tuple-element.149, f32[64,128,128]{2,1,0:T(8,128)} %convolution_multiply_fusion.4), kind=kCustom, calls=%fused_computation.8.clone.1 | custom fusion | flops 1048576 | bytes 12583168 | tf_op jit(solution)/shard_map/while/body/scatter-add | solution.py:35
  178.1 5.2 convolution_multiply_fusion.5
  183.3 8.8 %scatter_fusion.1 = f32[32,128,128]{2,1,0:T(8,128)S(1)} fusion(f32[32,128,128]{2,1,0:T(8,128)S(1)} %get-tuple-element.167, s32[64]{0:T(128)S(1)} %get-tuple-element.150, f32[64,128,128]{2,1,0:T(8,128)} %convolution_multiply_fusion.5), kind=kCustom, calls=%fused_computation.9.clone.1 | custom fusion | flops 1048576 | bytes 12583168 | tf_op jit(solution)/shard_map/while/body/scatter-add | solution.py:35
  195.7 4.9 convolution_multiply_fusion.4
  200.6 13.5 %scatter_fusion = f32[128,128,128]{2,1,0:T(8,128)} fusion(f32[128,128,128]{2,1,0:T(8,128)} %get-tuple-element.166, s32[64]{0:T(128)S(1)} %get-tuple-element.149, f32[64,128,128]{2,1,0:T(8,128)} %convolution_multiply_fusion.4), kind=kCustom, calls=%fused_computation.8.clone.1 | custom fusion | flops 1048576 | bytes 12583168 | tf_op jit(solution)/shard_map/while/body/scatter-add | solution.py:35
  218.5 5.2 convolution_multiply_fusion.5
  223.7 8.8 %scatter_fusion.1 = f32[32,128,128]{2,1,0:T(8,128)S(1)} fusion(f32[32,128,128]{2,1,0:T(8,128)S(1)} %get-tuple-element.167, s32[64]{0:T(128)S(1)} %get-tuple-element.150, f32[64,128,128]{2,1,0:T(8,128)} %convolution_multiply_fusion.5), kind=kCustom, calls=%fused_computation.9.clone.1 | custom fusion | flops 1048576 | bytes 12583168 | tf_op jit(solution)/shard_map/while/body/scatter-add | solution.py:35
  236.1 4.9 convolution_multiply_fusion.4
  241.0 13.6 %scatter_fusion = f32[128,128,128]{2,1,0:T(8,128)} fusion(f32[128,128,128]{2,1,0:T(8,128)} %get-tuple-element.166, s32[64]{0:T(128)S(1)} %get-tuple-element.149, f32[64,128,128]{2,1,0:T(8,128)} %convolution_multiply_fusion.4), kind=kCustom, calls=%fused_computation.8.clone.1 | custom fusion | flops 1048576 | bytes 12583168 | tf_op jit(solution)/shard_map/while/body/scatter-add | solution.py:35
  259.0 5.2 convolution_multiply_fusion.5
  264.2 8.8 %scatter_fusion.1 = f32[32,128,128]{2,1,0:T(8,128)S(1)} fusion(f32[32,128,128]{2,1,0:T(8,128)S(1)} %get-tuple-element.167, s32[64]{0:T(128)S(1)} %get-tuple-element.150, f32[64,128,128]{2,1,0:T(8,128)} %convolution_multiply_fusion.5), kind=kCustom, calls=%fused_computation.9.clone.1 | custom fusion | flops 1048576 | bytes 12583168 | tf_op jit(solution)/shard_map/while/body/scatter-add | solution.py:35
  274.2 6.3 convert_element_type.51
  286.0 164.8 %all-to-all-start = ((s32[32,1,32]{2,1,0:T(1,128)}), s32[32,1,32]{2,1,0:T(1,128)S(1)}, u32[]{:S(2)}, u32[]{:S(2)}) async-start(s32[32,1,32]{2,1,0:T(1,128)} %all_to_all.22), calls=%async_computation.2 | async-start | bytes 32768 | tf_op jit(solution)/shard_map/all_to_all | solution.py:90
  462.2 7.0 %all-to-all-done.2 = s32[32,1,32]{2,1,0:T(1,128)S(1)} async-done(((s32[32,1,32]{2,1,0:T(1,128)}), s32[32,1,32]{2,1,0:T(1,128)S(1)}, u32[]{:S(2)}, u32[]{:S(2)}) %all-to-all-start.2) | async-done | bytes 4128 | tf_op jit(solution)/shard_map/all_to_all | solution.py:93
  477.1 79.7 %reduce-scatter.3.cloned.1.call-done = bf16[2048,128]{1,0:T(8,128)(2,1)} async-done(((bf16[16384,128]{1,0:T(8,128)(2,1)}), bf16[2048,128]{1,0:T(8,128)(2,1)}) %reduce-scatter.3.cloned.1.call-update) | async-done | bytes 524304 | tf_op jit(solution)/shard_map/reduce_scatter | solution.py:73
  567.0 71.9 %all-gather = f32[1024,128]{1,0:T(8,128)S(1)} all-gather(f32[32,128]{1,0:T(8,128)S(1)} %gather_fusion.4), channel_id=2, replica_groups=mesh['row'=4,'col'=8] {'row','col'}, dimensions={0}, use_global_device_ids=true | all-gather | bytes 540672 | tf_op jit(solution)/shard_map/all_gather | solution.py:116
  (100 shorter events, 83.7 us)
Async XLA Ops:
  7.2 22.4 %all-gather.4.cloned.1.call-start = ((), (), s32[]{:S(2)}) async-start(), calls=%async_computation.6 | async-start | bytes 1310720 | tf_op jit(solution)/shard_map/all_gather | solution.py:67
  9.0 96.7 %all-gather.6.cloned.1.call-start = ((), (), s32[]{:S(2)}) async-start(), calls=%async_computation.7 | async-start | bytes 4718592 | tf_op jit(solution)/shard_map/all_gather | solution.py:66
  11.2 458.2 %reduce-scatter.5.cloned.1.call-start = ((), (), s32[]{:S(2)}) async-start(), calls=%async_computation.9 | async-start | bytes 1310720 | tf_op jit(solution)/shard_map/reduce_scatter | solution.py:76
  110.0 1.2 copy-start
  274.2 282.6 %reduce-scatter.3.cloned.1.call-start = ((), (), s32[]{:S(2)}) async-start(), calls=%async_computation.8 | async-start | bytes 4718592 | tf_op jit(solution)/shard_map/reduce_scatter | solution.py:73
  280.6 0.7 copy-start.5
  280.6 170.2 %copy-start.6 = (s32[512]{0:T(512)S(1)}, s32[512]{0:T(512)}, u32[]{:S(2)}) copy-start(s32[512]{0:T(512)} %param.18) | copy-start | bytes 6148
  280.6 188.8 %copy-start.4 = (f32[1,1,1024,128]{3,2,1,0:T(8,128)S(1)}, f32[1,1,1024,128]{3,2,1,0:T(8,128)}, u32[]{:S(2)}) copy-start(f32[1,1,1024,128]{3,2,1,0:T(8,128)} %param.12) | copy-start | bytes 1572868
  286.0 171.8 %all-to-all-start = ((s32[32,1,32]{2,1,0:T(1,128)}), s32[32,1,32]{2,1,0:T(1,128)S(1)}, u32[]{:S(2)}, u32[]{:S(2)}) async-start(s32[32,1,32]{2,1,0:T(1,128)} %all_to_all.22), calls=%async_computation.2 | async-start | bytes 32768 | tf_op jit(solution)/shard_map/all_to_all | solution.py:90
  457.8 11.4 %all-to-all-start.2 = ((s32[32,1,32]{2,1,0:T(1,128)}), s32[32,1,32]{2,1,0:T(1,128)S(1)}, u32[]{:S(2)}, u32[]{:S(2)}) async-start(s32[32,1,32]{2,1,0:T(1,128)} %all_to_all.26), calls=%async_computation.4 | async-start | bytes 32768 | tf_op jit(solution)/shard_map/all_to_all | solution.py:93
  469.3 87.5 %copy-start.3 = (f32[1,1,2048,128]{3,2,1,0:T(8,128)S(1)}, f32[1,1,2048,128]{3,2,1,0:T(8,128)}, u32[]{:S(2)}) copy-start(f32[1,1,2048,128]{3,2,1,0:T(8,128)} %param.11) | copy-start | bytes 3145732
  470.4 95.9 %copy-start.1 = (f32[1024,128]{1,0:T(8,128)}, f32[1024,128]{1,0:T(8,128)S(1)}, u32[]{:S(2)}) copy-start(f32[1024,128]{1,0:T(8,128)S(1)} %fusion.5) | copy-start | bytes 1572868
  474.5 87.5 %all-to-all-start.3 = ((bf16[32,32,128]{2,1,0:T(8,128)(2,1)}), bf16[32,32,128]{2,1,0:T(8,128)(2,1)S(1)}, u32[]{:S(2)}, u32[]{:S(2)}) async-start(bf16[32,32,128]{2,1,0:T(8,128)(2,1)} %bitcast.22), calls=%async_computation.5 | async-start | bytes 524288 | tf_op jit(solution)/shard_map/all_to_all | solution.py:103
  557.9 81.0 %copy-start.2 = (f32[2048,128]{1,0:T(8,128)}, f32[2048,128]{1,0:T(8,128)S(1)}, u32[]{:S(2)}) copy-start(f32[2048,128]{1,0:T(8,128)S(1)} %fusion.4) | copy-start | bytes 3145732
  562.0 77.9 %all-to-all-start.1 = ((bf16[32,32,128]{2,1,0:T(8,128)(2,1)}), bf16[32,32,128]{2,1,0:T(8,128)(2,1)S(1)}, u32[]{:S(2)}, u32[]{:S(2)}) async-start(bf16[32,32,128]{2,1,0:T(8,128)(2,1)} %bitcast.17), calls=%async_computation.3 | async-start | bytes 524288 | tf_op jit(solution)/shard_map/all_to_all | solution.py:96
Sparse Core Ops, SparseCore 0:
  10.1 19.4 all-gather.3
  32.3 73.3 all-gather.5
  274.3 185.2 reduce-scatter.4
  463.5 93.1 reduce-scatter.2
where the time goes:
time: 656 us; the launch traced here: 652 us
  waiting for transfers between devices  182 us (28%)
  starting transfers between devices  176 us (27%)
  other arithmetic  113 us (17%)
  blocking collectives  71.9 us (11%)
  local copies, waits for them, and re-layouts  51 us (8%)
  matrix products  43.5 us (7%)
  between operations  14.7 us (2%)
    all_to_all x1, starting transfers between devices, on_device(): lax.all_to_all(user_request, ('row', 'col'), split_axis=0, concat_axis=0,...  165 us
    reduce_scatter x1, waiting for transfers between devices, on_device(): lax.psum_scatter(user_part.reshape(-1, embed).astype(jnp.bfloat16), 'col'...  79.7 us
    all_gather x1, waiting for transfers between devices, on_device(): lax.all_gather(user_emb.astype(jnp.bfloat16), 'col', axis=1, tiled=True)  76.1 us
    all_gather x1, blocking collectives, on_device(): lax.all_gather(item_final[mine], ('row', 'col'), axis=0, tiled=True)  71.9 us
    scatter-add x4, other arithmetic, advance(): user_part.at[row_ids].add(to_users)  54.4 us
    scatter-add x4, other arithmetic, advance(): item_part.at[col_ids].add(to_items)  35.2 us
    dot_general x4, matrix products, advance(): jnp.einsum('tij,tie->tje', values, user_tiles[row_ids], preferred_element...  20.9 us
    dot_general x4, matrix products, advance(): jnp.einsum('tij,tje->tie', values, item_tiles[col_ids], preferred_element...  19.6 us
  transfers between devices with their start and end apart: 8, of which 5 were waited for; matrix products, arithmetic and copies ran while one was open for 5% of the time, Pallas kernels for 0%

commit v1 on v0

v1 whole, which is shorter than its diff:
```python
import functools

import jax
import jax.numpy as jnp
from jax import lax
from jax.experimental import pallas as pl
from jax.experimental.pallas import tpu as pltpu
from jax.sharding import PartitionSpec as P

F32 = jnp.float32
BF16 = jnp.bfloat16
VMEM_WHOLE = pl.BlockSpec(memory_space=pltpu.VMEM)


def split_axis(size):
    fast = max(d for d in range(1, size + 1) if size % d == 0 and d * d <= size)
    return size // fast, fast


def arrivals(slow):
    return [sorted(range(slow), key=lambda t: (abs(t - z), t < z)) for z in range(slow)]


def moves(slow, fast, step):
    pairs = []
    for z in range(slow):
        for x in range(fast):
            to = step(z, x)
            if to is not None:
                pairs.append((z * fast + x, to[0] * fast + to[1]))
    return pairs


def choose(place, options):
    picked = None
    seen = []
    for z, option in enumerate(options):
        if option is None or any(option is other for other, _ in seen):
            continue
        seen.append((option, [i for i, o in enumerate(options) if o is option]))
    for option, places in seen:
        if picked is None:
            picked = option
            continue
        here = functools.reduce(jnp.logical_or, [place == i for i in places])
        picked = jnp.where(here, option, picked)
    return picked


def group_of(slots):
    return next(g for g in (32, 16, 8, 4, 2, 1) if slots % g == 0)


def add_tiles(count, first, group, unroll, left, right, place, trash, total):
    live = jnp.clip(count - first, 0, group)

    def some(step, carry):
        products, places = [], []
        for u in range(unroll):
            slot = step * unroll + u
            whole = first + slot
            products.append(jnp.dot(left(slot, whole), right(slot, whole), preferred_element_type=F32))
            places.append(jnp.where(slot < live, place(whole), trash))
        for product, at in zip(products, places):
            total[at] += product
        return carry

    lax.fori_loop(0, (live + unroll - 1) // unroll, some, 0)


def user_term_kernel(count_ref, rows_ref, cols_ref, base_ref, vals_ref, item_ref, *rest, group, unroll, trash):
    *outs, total = rest
    step = pl.program_id(0)

    @pl.when(step == 0)
    def _():
        total[...] = jnp.zeros_like(total)

    add_tiles(
        count_ref[0],
        step * group,
        group,
        unroll,
        lambda slot, whole: vals_ref[slot],
        lambda slot, whole: item_ref[cols_ref[whole]],
        lambda whole: rows_ref[whole],
        trash,
        total,
    )

    @pl.when(step == pl.num_programs(0) - 1)
    def _():
        for n, out in enumerate(outs):

            def tile(i, carry, n=n, out=out):
                out[i] = total[base_ref[n] + i].astype(BF16)
                return carry

            lax.fori_loop(0, out.shape[0], tile, 0, unroll=2)


def item_term_kernel(count_ref, rows_ref, cols_ref, in_base_ref, out_base_ref, vals_ref, *rest, blocks, group, unroll, trash):
    users = rest[:blocks]
    outs = rest[blocks:-3]
    table, total, sems = rest[-3:]
    step = pl.program_id(0)

    @pl.when(step == 0)
    def _():
        copies = [
            pltpu.make_async_copy(user, table.at[pl.ds(in_base_ref[n], user.shape[0])], sems.at[n])
            for n, user in enumerate(users)
        ]
        for copy in copies:
            copy.start()
        total[...] = jnp.zeros_like(total)
        for copy in copies:
            copy.wait()

    add_tiles(
        count_ref[0],
        step * group,
        group,
        unroll,
        lambda slot, whole: table[rows_ref[whole]],
        lambda slot, whole: vals_ref[slot],
        lambda whole: cols_ref[whole],
        trash,
        total,
    )

    @pl.when(step == pl.num_programs(0) - 1)
    def _():
        for n, out in enumerate(outs):

            def tile(i, carry, n=n, out=out):
                out[i] = total[out_base_ref[n] + i].astype(BF16)
                return carry

            lax.fori_loop(0, out.shape[0], tile, 0, unroll=2)


def values_spec(group, side):
    def where(i, count, *_):
        return (jnp.minimum(i, jnp.maximum(count[0] - 1, 0) // group), 0, 0)

    return pl.BlockSpec((group, side, side), where)


def user_terms(count, rows, cols, base, vals, items, tiles, outs, out_tiles):
    slots, side = vals.shape[0], vals.shape[1]
    embed = items.shape[-1]
    group = group_of(slots)
    unroll = min(8, group)
    return pl.pallas_call(
        functools.partial(user_term_kernel, group=group, unroll=unroll, trash=tiles),
        grid_spec=pltpu.PrefetchScalarGridSpec(
            num_scalar_prefetch=4,
            grid=(slots // group,),
            in_specs=[values_spec(group, side), pl.BlockSpec(items.shape, lambda i, *_: (0, 0, 0))],
            out_specs=[pl.BlockSpec((out_tiles, side, embed), lambda i, *_: (0, 0, 0)) for _ in range(outs)],
            scratch_shapes=[pltpu.VMEM((tiles + 1, side, embed), F32)],
        ),
        out_shape=[jax.ShapeDtypeStruct((out_tiles, side, embed), BF16) for _ in range(outs)],
        compiler_params=pltpu.CompilerParams(
            dimension_semantics=("arbitrary",), vmem_limit_bytes=32 * 2**20
        ),
        cost_estimate=pl.CostEstimate(
            flops=2 * slots * side * side * embed, bytes_accessed=2 * slots * side * side, transcendentals=0
        ),
        name="user_terms",
    )(count, rows, cols, base, vals, items)


def item_terms(count, rows, cols, in_base, out_base, vals, users, tiles, outs, out_tiles):
    slots, side = vals.shape[0], vals.shape[1]
    embed = users[0].shape[1]
    group = group_of(slots)
    unroll = min(8, group)
    table = len(users) * users[0].shape[0]
    return pl.pallas_call(
        functools.partial(item_term_kernel, blocks=len(users), group=group, unroll=unroll, trash=tiles),
        grid_spec=pltpu.PrefetchScalarGridSpec(
            num_scalar_prefetch=5,
            grid=(slots // group,),
            in_specs=[values_spec(group, side)] + [pl.BlockSpec(memory_space=pl.ANY) for _ in users],
            out_specs=[pl.BlockSpec((out_tiles, embed, side), lambda i, *_: (0, 0, 0)) for _ in range(outs)],
            scratch_shapes=[
                pltpu.VMEM((table, embed, side), BF16),
                pltpu.VMEM((tiles + 1, embed, side), F32),
                pltpu.SemaphoreType.DMA((len(users),)),
            ],
        ),
        out_shape=[jax.ShapeDtypeStruct((out_tiles, embed, side), BF16) for _ in range(outs)],
        compiler_params=pltpu.CompilerParams(
            dimension_semantics=("arbitrary",), vmem_limit_bytes=32 * 2**20
        ),
        cost_estimate=pl.CostEstimate(
            flops=2 * slots * side * side * embed, bytes_accessed=2 * slots * side * side, transcendentals=0
        ),
        name="item_terms",
    )(count, rows, cols, in_base, out_base, vals, *users)


def picked_rows(wanted_ref, low, out_ref, chunk):
    rows = low.shape[0]
    for at in range(0, wanted_ref.shape[0], chunk):
        some = min(chunk, wanted_ref.shape[0] - at)
        hot = wanted_ref[pl.ds(at, some), :] == lax.broadcasted_iota(jnp.int32, (some, rows), 1)
        out_ref[pl.ds(at, some), :] = jnp.dot(hot.astype(BF16), low, preferred_element_type=F32).astype(BF16)


def combine_kernel(emb_ref, wanted_ref, *rest, terms, transposed):
    parts = rest[:terms]
    final_ref, rows_ref = rest[terms:]
    side = parts[0].shape[-2]
    for i in range(parts[0].shape[0]):
        at = pl.ds(i * side, side)
        prop = functools.reduce(jnp.add, [part[i].astype(F32) for part in parts])
        if transposed:
            prop = prop.T
        final_ref[at, :] = (emb_ref[at, :] + prop) * 0.5
    picked_rows(wanted_ref, final_ref[...].astype(BF16), rows_ref, 256)


def combine(emb, parts, wanted, transposed, name):
    return pl.pallas_call(
        functools.partial(combine_kernel, terms=len(parts), transposed=transposed),
        in_specs=[VMEM_WHOLE] * (2 + len(parts)),
        out_specs=[VMEM_WHOLE] * 2,
        out_shape=[
            jax.ShapeDtypeStruct(emb.shape, F32),
            jax.ShapeDtypeStruct((wanted.shape[0], emb.shape[1]), BF16),
        ],
        compiler_params=pltpu.CompilerParams(vmem_limit_bytes=32 * 2**20),
        name=name,
    )(emb, wanted, *parts)


def bpr_kernel(user_slot_ref, item_slot_ref, users_ref, items_ref, negatives_ref, out_ref):
    def vectors(slot_ref, rows_ref):
        hot = slot_ref[...] == lax.broadcasted_iota(jnp.int32, (slot_ref.shape[0], rows_ref.shape[0]), 1)
        return jnp.dot(hot.astype(BF16), rows_ref[...], preferred_element_type=F32)

    users = vectors(user_slot_ref, users_ref)
    items = vectors(item_slot_ref, items_ref)
    positive = jnp.sum(users * items, axis=1, keepdims=True)
    against = lax.dot_general(
        users.astype(BF16), negatives_ref[...], (((1,), (1,)), ((), ())), preferred_element_type=F32
    )
    out_ref[...] = jnp.log1p(jnp.exp(against - positive))


def bpr(user_slot, item_slot, users, items, negatives):
    pairs, embed = user_slot.shape[0], users.shape[1]
    block = next(b for b in (128, 64, 32, 16, 8, pairs) if pairs % b == 0)
    whole = lambda array: pl.BlockSpec(array.shape, lambda i: (0, 0))
    return pl.pallas_call(
        bpr_kernel,
        grid=(pairs // block,),
        in_specs=[pl.BlockSpec((block, 1), lambda i: (i, 0))] * 2 + [whole(users), whole(items), whole(negatives)],
        out_specs=pl.BlockSpec((block, negatives.shape[0]), lambda i: (i, 0)),
        out_shape=jax.ShapeDtypeStruct((pairs, negatives.shape[0]), F32),
        compiler_params=pltpu.CompilerParams(
            dimension_semantics=("arbitrary",), vmem_limit_bytes=32 * 2**20
        ),
        name="bpr_terms",
    )(user_slot, item_slot, users, items, negatives)


def place_requests(owner, local, slots):
    pairs = owner.shape[0]
    order = jnp.arange(pairs, dtype=jnp.int32)
    same = (owner[:, None] == owner[None, :]) & (order[None, :] < order[:, None])
    slot = owner * slots + jnp.sum(same.astype(jnp.int32), axis=1)
    return slot


def requests_of(slot, local, total):
    hits = slot[:, None] == jnp.arange(total, dtype=jnp.int32)[None, :]
    return jnp.sum(jnp.where(hits, local[:, None], 0), axis=0)


def on_device(user_emb, item_emb, tile_vals, tile_rows, tile_cols, tile_count, pair_users, pair_items, negatives):
    row_count, col_count = lax.axis_size("row"), lax.axis_size("col")
    row, col = lax.axis_index("row"), lax.axis_index("col")
    devices = row_count * col_count
    user_dev, embed = user_emb.shape[2:]
    item_dev = item_emb.shape[2]
    side = tile_vals.shape[-1]
    user_tiles, item_tiles = user_dev // side, item_dev // side
    slow, fast = split_axis(col_count)
    z, x = col // fast, col % fast
    row_slow, row_fast = split_axis(row_count) if row_count % 2 else (row_count // 2, 2)
    y, core = row // row_fast, row % row_fast

    user_mine, item_mine = user_emb[0, 0], item_emb[0, 0]
    count, rows, cols = tile_count[0], tile_rows[0, 0], tile_cols[0, 0]
    vals = tile_vals[0, 0]
    user_low = jnp.swapaxes(user_mine.astype(BF16).reshape(user_tiles, side, embed), 1, 2)
    item_low = item_mine.astype(BF16).reshape(item_tiles, side, embed)

    def send_col(array, step):
        return lax.ppermute(array, "col", moves(slow, fast, step))

    def send_row(array, step):
        return lax.ppermute(array, "row", moves(row_slow, row_fast, step))

    halves = [item_low]
    for j in range(1, row_slow):
        halves.append(send_row(item_low, lambda a, b, j=j: ((a + j) % row_slow, b)))
    item_blocks = {(j, 0): half for j, half in enumerate(halves)}
    for i in range(1, row_fast):
        for j, half in enumerate(halves):
            item_blocks[j, i] = send_row(half, lambda a, b, i=i: (a, (b + i) % row_fast))
    item_parts = jnp.stack([item_blocks[j, i] for j in range(row_slow) for i in range(row_fast)])
    item_order = jnp.stack(
        [
            (y - row_id // row_fast) % row_slow * row_fast + (core - row_id % row_fast) % row_fast
            for row_id in range(row_count)
        ]
    )
    item_table = item_parts.reshape(row_count * item_tiles, side, embed)
    col_owner, col_within = cols // item_tiles, cols % item_tiles
    owner_y, owner_core = col_owner // row_fast, col_owner % row_fast
    near_cols = ((y - owner_y) % row_slow * row_fast + (core - owner_core) % row_fast) * item_tiles + col_within

    order = arrivals(slow)
    up, down = {0: user_low}, {0: user_low}
    user_blocks = []
    order_table = jnp.asarray(order, jnp.int32)
    for k in range(slow):
        if k:
            up[k] = send_col(up[k - 1], lambda a, b, k=k: (a + 1, b) if k - 1 <= a < slow - 1 else None)
            down[k] = send_col(down[k - 1], lambda a, b, k=k: (a - 1, b) if 0 < a <= slow - k else None)
    for k in range(slow):
        sources = []
        for place in range(slow):
            other = order[place][k]
            sources.append(up[place - other] if other <= place else down[other - place])
        block = choose(z, sources)
        user_blocks.append((block, order_table[z, k] * fast + x))
        for j in range(1, fast):
            moved = send_col(block, lambda a, b, j=j: (a, (b + j) % fast))
            user_blocks.append((moved, order_table[z, k] * fast + (x - j) % fast))
    in_base = jnp.stack([place for _, place in user_blocks]) * user_tiles

    out_places = []
    for k in range(slow):
        for j in range(fast):
            out_places.append(order_table[z, slow - 1 - k] * fast + (x + j) % fast)
    out_base = jnp.stack(out_places) * user_tiles
    user_parts = user_terms(
        count, rows, near_cols, out_base, vals, item_table, col_count * user_tiles, col_count, user_tiles
    )
    sums = []
    for k in range(slow):
        keep = user_parts[k * fast]
        others = [
            send_col(user_parts[k * fast + j], lambda a, b, j=j: (a, (b + j) % fast)) for j in range(1, fast)
        ]
        if k < slow - 1:
            total = functools.reduce(jnp.add, [part.astype(F32) for part in [keep] + others]).astype(BF16)
            sums.append(total)
        else:
            sums.append([keep] + others)
    rising = falling = None
    for step in range(1, slow):
        far = slow - step

        def onward(sign, before, far=far):
            picks = []
            for place in range(slow):
                target = place + sign * far
                picks.append(sums[slow - 1 - order[place].index(target)] if 0 <= target < slow else None)
            mine = choose(z, picks)
            if before is not None:
                mine = (mine.astype(F32) + before.astype(F32)).astype(BF16)
            return send_col(mine, lambda a, b: (a + sign, b) if 0 <= a + sign * far < slow else None)

        rising, falling = onward(1, rising), onward(-1, falling)
    user_terms_in = sums[-1] + ([rising, falling] if slow > 1 else [])

    item_places = [
        (y + j) % row_slow * row_fast + (core + i) % row_fast for j in range(row_slow) for i in range(row_fast)
    ]
    item_base = jnp.stack(item_places) * item_tiles
    item_out = item_terms(
        count,
        rows,
        cols,
        in_base,
        item_base,
        vals,
        [block for block, _ in user_blocks],
        row_count * item_tiles,
        row_count,
        item_tiles,
    )
    item_sums = []
    for j in range(row_slow):
        mine = [item_out[j * row_fast]] + [
            send_row(item_out[j * row_fast + i], lambda a, b, i=i: (a, (b + i) % row_fast))
            for i in range(1, row_fast)
        ]
        if j:
            total = functools.reduce(jnp.add, [part.astype(F32) for part in mine]).astype(BF16)
            item_sums.append(send_row(total, lambda a, b, j=j: ((a + j) % row_slow, b)))
        else:
            item_sums += mine

    slots = 2 * pair_users.shape[0] // devices
    user_owner, user_local = pair_users // user_dev, pair_users % user_dev
    item_holder, item_local = pair_items // item_dev, pair_items % item_dev
    item_owner = item_holder % row_count * col_count + item_holder // row_count
    user_slot = place_requests(user_owner, user_local, slots)
    item_slot = place_requests(item_owner, item_local, slots)
    asked = jnp.stack(
        [
            requests_of(user_slot, user_local, devices * slots).reshape(devices, slots),
            requests_of(item_slot, item_local, devices * slots).reshape(devices, slots),
        ],
        axis=1,
    )
    wanted = lax.all_to_all(asked, ("row", "col"), split_axis=0, concat_axis=0, tiled=True)
    neg_each = negatives.shape[0] // devices
    offset = (col * row_count + row) * item_dev
    named = lax.dynamic_slice_in_dim(negatives, (row * col_count + col) * neg_each, neg_each, 0) - offset

    user_wanted = wanted[:, 0].reshape(-1, 1)
    item_wanted = jnp.concatenate([wanted[:, 1].reshape(-1), named]).reshape(-1, 1)

    item_final, item_rows = combine(item_mine, item_sums, item_wanted, True, "item_final")
    asked_rows = item_rows[: devices * slots].reshape(devices, slots, embed)
    named_rows = jnp.broadcast_to(item_rows[None, devices * slots :], (devices, neg_each, embed))
    item_back = lax.all_to_all(
        jnp.concatenate([asked_rows, named_rows], axis=1), ("row", "col"), split_axis=0, concat_axis=0, tiled=True
    )
    item_table_back = item_back[:, :slots].reshape(devices * slots, embed)
    negative_rows = item_back[:, slots:].reshape(devices * neg_each, embed)

    user_final, user_rows = combine(user_mine, user_terms_in, user_wanted, False, "user_final")
    user_back = lax.all_to_all(
        user_rows.reshape(devices, slots, embed), ("row", "col"), split_axis=0, concat_axis=0, tiled=True
    ).reshape(devices * slots, embed)
    bpr_terms = bpr(user_slot[:, None], item_slot[:, None], user_back, item_table_back, negative_rows)
    return user_final.reshape(user_emb.shape), item_final.reshape(item_emb.shape), bpr_terms


def solution(mesh):
    placed = (
        P("row", "col", None, None),
        P("col", "row", None, None),
        P("row", "col", None, None, None),
        P("row", "col", None),
        P("row", "col", None),
        P("row", "col"),
        P(("row", "col")),
        P(("row", "col")),
        P(),
    )
    return jax.shard_map(
        on_device,
        mesh=mesh,
        in_specs=placed,
        out_specs=(
            P("row", "col", None, None),
            P("col", "row", None, None),
            P(("row", "col"), None),
        ),
        check_vma=False,
    )
```

time: 656 us -> 217 us (0.33)
  starting transfers between devices: 176 us -> 55.5 us
  other arithmetic: 113 us -> 14.5 us
  waiting for transfers between devices: 182 us -> 84.4 us
  blocking collectives: 71.9 us -> 0 us
  matrix products: 43.5 us -> 0 us
  Pallas kernels: 0 us -> 40.5 us
  local copies, waits for them, and re-layouts: 51 us -> 15.2 us
  between operations: 14.7 us -> 4.65 us
    all_to_all x4 -> x3, starting transfers between devices: 176 us -> 14.1 us  [the longest x1 5.33 us: on_device(): lax.all_to_all(asked, ('row', 'col'), split_axis=0, concat_axis=0, tiled=...]
    all_gather x2 -> x0, waiting for transfers between devices: 93.8 us -> none  [the longest x1 76.1 us: on_device(): lax.all_gather(user_emb.astype(jnp.bfloat16), 'col', axis=1, tiled=True)]
    scatter-add x8 -> x0, other arithmetic: 89.6 us -> none  [the longest x4 54.4 us: advance(): user_part.at[row_ids].add(to_users)]
    reduce_scatter x2 -> x0, waiting for transfers between devices: 79.7 us -> none  [the longest x1 79.7 us: on_device(): lax.psum_scatter(user_part.reshape(-1, embed).astype(jnp.bfloat16), 'col'...]
    ppermute x0 -> x26, waiting for transfers between devices: none -> 75.2 us  [the longest x20 69.7 us: send_col(): return lax.ppermute(array, 'col', moves(slow, fast, step))]
    all_gather x1 -> x0, blocking collectives: 71.9 us -> none  [on_device(): lax.all_gather(item_final[mine], ('row', 'col'), axis=0, tiled=True)]
    dot_general x9 -> x0, matrix products: 43.5 us -> none  [the longest x4 20.9 us: advance(): jnp.einsum('tij,tie->tje', values, user_tiles[row_ids], preferred_element...]
    ppermute x0 -> x26, starting transfers between devices: none -> 41.4 us  [the longest x20 37.5 us: send_col(): return lax.ppermute(array, 'col', moves(slow, fast, step))]
  transfers between devices with their start and end apart: 8 -> 29, of which waited for: 5 -> 11; matrix products, arithmetic and copies ran while one was open for 5% -> 8% of each run, Pallas kernels for 0% -> 17%
where the time goes in v1:
time: 217 us; the launch traced here: 215 us
  waiting for transfers between devices  84.4 us (39%)
  starting transfers between devices  55.5 us (26%)
  Pallas kernels  40.5 us (19%)
  local copies, waits for them, and re-layouts  15.2 us (7%)
  other arithmetic  14.5 us (7%)
  between operations  4.65 us (2%)
    ppermute x20, waiting for transfers between devices, send_col(): return lax.ppermute(array, 'col', moves(slow, fast, step))  69.7 us
    ppermute x20, starting transfers between devices, send_col(): return lax.ppermute(array, 'col', moves(slow, fast, step))  37.5 us
    pallas_call x1, Pallas kernels, item_terms(): pl.pallas_call(functools.partial(item_term_kernel, blocks=len(users), gro...  16.4 us
    pallas_call x1, Pallas kernels, user_terms(): pl.pallas_call(functools.partial(user_term_kernel, group=group, unroll=un...  16.2 us
    unnamed x40, local copies, waits for them, and re-layouts  11.6 us
    all_to_all x1, waiting for transfers between devices, on_device(): lax.all_to_all(user_rows.reshape(devices, slots, embed), ('row', 'col'),...  9.26 us
    ppermute x6, waiting for transfers between devices, send_row(): return lax.ppermute(array, 'row', moves(row_slow, row_fast, step))  5.52 us
    all_to_all x1, starting transfers between devices, on_device(): lax.all_to_all(asked, ('row', 'col'), split_axis=0, concat_axis=0, tiled=...  5.33 us
  transfers between devices with their start and end apart: 29, of which 11 were waited for; matrix products, arithmetic and copies ran while one was open for 8% of the time, Pallas kernels for 17%

profile of v1, /device:TPU:0, one launch (start us, length us, event | category | flops | bytes accessed | tf_op | source)
XLA Modules:
  0.0 214.8 jit_solution(7314141496140091273)
XLA Ops:
  2.3 5.0 %collective-permute-start.14 = (bf16[16,128,128]{2,1,0:T(8,128)(2,1)S(1)}, bf16[16,128,128]{2,1,0:T(8,128)(2,1)S(1)}, u32[]{:S(2)}, u32[]{:S(2)}) collective-permute-start(bf16[16,128,128]{2,1,0:T(8,128)(2,1)S(1)} %bitcast.54), channel_id=1, source_target_pairs={{0,2},{1,3},{2,4},{3,5},{4,6},{5,7},{8,10},{9,11},{10,12},{11,13},... | collective-permute-start | bytes 1572872 | tf_op jit(solution)/shard_map/ppermute | solution.py:304
  12.1 6.3 %collective-permute-done.14 = bf16[16,128,128]{2,1,0:T(8,128)(2,1)S(1)} collective-permute-done((bf16[16,128,128]{2,1,0:T(8,128)(2,1)S(1)}, bf16[16,128,128]{2,1,0:T(8,128)(2,1)S(1)}, u32[]{:S(2)}, u32[]{:S(2)}) %collective-permute-start.14) | collective-permute-done | bytes 524320 | tf_op jit(solution)/shard_map/ppermute | solution.py:304
  19.1 3.5 %collective-permute-done.15 = bf16[16,128,128]{2,1,0:T(8,128)(2,1)S(1)} collective-permute-done((bf16[16,128,128]{2,1,0:T(8,128)(2,1)S(1)}, bf16[16,128,128]{2,1,0:T(8,128)(2,1)S(1)}, u32[]{:S(2)}, u32[]{:S(2)}) %collective-permute-start.15) | collective-permute-done | bytes 524320 | tf_op jit(solution)/shard_map/ppermute | solution.py:304
  29.3 8.0 %collective-permute-done.18 = bf16[16,128,128]{2,1,0:T(8,128)(2,1)} collective-permute-done((bf16[16,128,128]{2,1,0:T(8,128)(2,1)S(1)}, bf16[16,128,128]{2,1,0:T(8,128)(2,1)}, u32[]{:S(2)}, u32[]{:S(2)}) %collective-permute-start.18) | collective-permute-done | bytes 524320 | tf_op jit(solution)/shard_map/ppermute | solution.py:304
  39.8 5.8 %copy-done = bf16[1,1,512,128,128]{4,3,2,1,0:T(8,128)(2,1)S(1)} copy-done((bf16[1,1,512,128,128]{4,3,2,1,0:T(8,128)(2,1)S(1)}, bf16[1,1,512,128,128]{4,3,2,1,0:T(8,128)(2,1)}, u32[]{:S(2)}) %copy-start) | copy-done | bytes 16777240
  45.5 16.2 %user_terms.1 = (bf16[16,128,128]{2,1,0:T(8,128)(2,1)S(1)}, bf16[16,128,128]{2,1,0:T(8,128)(2,1)}, bf16[16,128,128]{2,1,0:T(8,128)(2,1)S(1)}, bf16[16,128,128]{2...) custom-call(s32[1]{0:T(128)} %bitcast.47.count_ref, ...), custom_call_target="tpu_custom_call" | custom-call | flops 2147483648 | bytes 16777216 | tf_op jit(solution)/shard_map/user_terms/pallas_call | solution.py:155
  66.7 5.3 %all-to-all-start = ((s32[32,2,32]{2,1,0:T(2,128)}), s32[32,2,32]{2,1,0:T(2,128)S(1)}, u32[]{:S(2)}, u32[]{:S(2)}) async-start(s32[32,2,32]{2,1,0:T(2,128)} %pad_add_fusion), calls=%async_computation | async-start | bytes 65536 | tf_op jit(solution)/shard_map/all_to_all | solution.py:425
  79.2 9.3 %collective-permute-done.16.rest_3_ = bf16[16,128,128]{2,1,0:T(8,128)(2,1)} collective-permute-done((bf16[16,128,128]{2,1,0:T(8,128)(2,1)S(1)}, bf16[16,128,128]{2,1,0:T(8,128)(2,1)}, u32[]{:S(2)}, u32[]{:S(2)}) %collective-permute-start.16) | collective-permute-done | bytes 524320 | tf_op jit(solution)/shard_map/ppermute | solution.py:304
  88.5 5.4 %collective-permute-start.7 = (bf16[16,128,128]{2,1,0:T(8,128)(2,1)S(1)}, bf16[16,128,128]{2,1,0:T(8,128)(2,1)S(1)}, u32[]{:S(2)}, u32[]{:S(2)}) collective-permute-start(bf16[16,128,128]{2,1,0:T(8,128)(2,1)S(1)} %add_convert_fusion.5), channel_id=1, source_target_pairs={{0,2},{1,3},{8,10},{9,11},{16,18},{17,19},{24,26},{25,27}} | collective-permute-start | bytes 1572872 | tf_op jit(solution)/shard_map/ppermute | solution.py:304
  94.0 16.9 %collective-permute-done.19.rest_5_ = bf16[16,128,128]{2,1,0:T(8,128)(2,1)S(1)} collective-permute-done((bf16[16,128,128]{2,1,0:T(8,128)(2,1)S(1)}, bf16[16,128,128]{2,1,0:T(8,128)(2,1)S(1)}, u32[]{:S(2)}, u32[]{:S(2)}) %collective-permute-start.19) | collective-permute-done | bytes 524320 | tf_op jit(solution)/shard_map/ppermute | solution.py:304
  111.0 11.2 %collective-permute-done.22.rest_7_ = bf16[16,128,128]{2,1,0:T(8,128)(2,1)S(1)} collective-permute-done((bf16[16,128,128]{2,1,0:T(8,128)(2,1)S(1)}, bf16[16,128,128]{2,1,0:T(8,128)(2,1)S(1)}, u32[]{:S(2)}, u32[]{:S(2)}) %collective-permute-start.22) | collective-permute-done | bytes 524320 | tf_op jit(solution)/shard_map/ppermute | solution.py:304
  122.2 5.8 %copy-done.1 = bf16[1,1,512,128,128]{4,3,2,1,0:T(8,128)(2,1)S(1)} copy-done((bf16[1,1,512,128,128]{4,3,2,1,0:T(8,128)(2,1)S(1)}, bf16[1,1,512,128,128]{4,3,2,1,0:T(8,128)(2,1)}, u32[]{:S(2)}) %copy-start.1) | copy-done | bytes 16777240
  128.0 16.4 %item_terms.1 = (bf16[8,128,128]{2,1,0:T(8,128)(2,1)S(1)}, bf16[8,128,128]{2,1,0:T(8,128)(2,1)}, bf16[8,128,128]{2,1,0:T(8,128)(2,1)S(1)}, bf16[8,128,128]{2,1,0:T(8,128)(2,1)S(1)}) custom-call(s32[1]{0:T(128)} %bitcast.48.count_ref, s32[512]{0:T(512)S(1)} %bitcast.62, s32[512]{0:T(512)S(1)} %bitcast.64, s32[8]{0:T(128)S(1)} %broadcast_multiply_fusion.in_base_ref, ...), custom_call_target="tpu_custom_call" | custom-call | flops 2147483648 | bytes 16777216 | tf_op jit(solution)/shard_map/item_terms/pallas_call | solution.py:181
  147.4 6.4 %collective-permute-start.8 = (bf16[16,128,128]{2,1,0:T(8,128)(2,1)}, bf16[16,128,128]{2,1,0:T(8,128)(2,1)}, u32[]{:S(2)}, u32[]{:S(2)}) collective-permute-start(bf16[16,128,128]{2,1,0:T(8,128)(2,1)} %get-tuple-element.38), channel_id=1, source_target_pairs={{0,2},{1,3},{2,4},{3,5},{8,10},{9,11},{10,12},{11,13},{16,18},{17,... | collective-permute-start | bytes 1572872 | tf_op jit(solution)/shard_map/ppermute | solution.py:304
  157.3 5.5 %collective-permute-done.25.rest_2_ = bf16[8,128,128]{2,1,0:T(8,128)(2,1)S(1)} collective-permute-done((bf16[8,128,128]{2,1,0:T(8,128)(2,1)S(1)}, bf16[8,128,128]{2,1,0:T(8,128)(2,1)S(1)}, u32[]{:S(2)}, u32[]{:S(2)}) %collective-permute-start.25) | collective-permute-done | bytes 262176 | tf_op jit(solution)/shard_map/ppermute | solution.py:307
  164.8 3.6 %all-to-all-start.2 = ((bf16[32,64,128]{2,1,0:T(8,128)(2,1)}), bf16[32,64,128]{2,1,0:T(8,128)(2,1)}, u32[]{:S(2)}, u32[]{:S(2)}) async-start(bf16[32,64,128]{2,1,0:T(8,128)(2,1)} %pad_maximum_fusion.1), calls=%async_computation.2 | async-start | bytes 1048576 | tf_op jit(solution)/shard_map/all_to_all | solution.py:436
  170.2 3.2 %add_convert_fusion = (bf16[16,128,128]{2,1,0:T(8,128)(2,1)}, bf16[16,128,128]{2,1,0:T(8,128)(2,1)}) fusion(bf16[16,128,128]{2,1,0:T(8,128)(2,1)} %collective-permute-done.11, pred[]{:T(512)S(6)} %eq.112, bf16[16,128,128]{2,1,0:T(8,128)(2,1)} %collective-permute-done.4, bf16[16,128,128]{2,1,0:T(8,128)(2,1)S(1)} %copy-done.7, ...), kind=kLoop, calls=%fused_computation.5 | loop fusion | flops 4456448 | bytes 4194305 | tf_op jit(solution)/shard_map/convert_element_type | solution.py:378
  174.7 5.4 %collective-permute-start.9 = (bf16[16,128,128]{2,1,0:T(8,128)(2,1)}, bf16[16,128,128]{2,1,0:T(8,128)(2,1)}, u32[]{:S(2)}, u32[]{:S(2)}) collective-permute-start(bf16[16,128,128]{2,1,0:T(8,128)(2,1)} %get-tuple-element.42), channel_id=1, source_target_pairs={{0,2},{1,3},{2,4},{3,5},{4,6},{5,7},{8,10},{9,11},{10,12},{11,13},... | collective-permute-start | bytes 1572872 | tf_op jit(solution)/shard_map/ppermute | solution.py:304
  180.6 7.4 %collective-permute-done.3.rest_1_ = bf16[16,128,128]{2,1,0:T(8,128)(2,1)S(1)} collective-permute-done((bf16[16,128,128]{2,1,0:T(8,128)(2,1)}, bf16[16,128,128]{2,1,0:T(8,128)(2,1)S(1)}, u32[]{:S(2)}, u32[]{:S(2)}) %collective-permute-start.3) | collective-permute-done | bytes 524320 | tf_op jit(solution)/shard_map/ppermute | solution.py:304
  188.0 4.2 %collective-permute-done.12.rest_3_ = bf16[16,128,128]{2,1,0:T(8,128)(2,1)S(1)} collective-permute-done((bf16[16,128,128]{2,1,0:T(8,128)(2,1)}, bf16[16,128,128]{2,1,0:T(8,128)(2,1)S(1)}, u32[]{:S(2)}, u32[]{:S(2)}) %collective-permute-start.12) | collective-permute-done | bytes 524320 | tf_op jit(solution)/shard_map/ppermute | solution.py:304
  192.2 3.3 %user_final.1 = (f32[2048,128]{1,0:T(8,128)}, bf16[1024,128]{1,0:T(8,128)(2,1)}) custom-call(f32[2048,128]{1,0:T(8,128)S(1)} %bitcast.51, s32[1024,1]{1,0:T(8,128)S(1)} %reshape_squeeze.8.wanted_ref, bf16[16,128,128]{2,1,0:T(8,128)(2,1)S(1)} %copy-done.5, bf16[16,128,128]{2,1,0:T(8,128)(2,1)S(1)} %collective-permute-done.3.rest_1_, ...), custom_call_target="tpu_custom_call" | custom-call | tf_op jit(solution)/shard_map/user_final/pallas_call | solution.py:227
  195.4 5.2 %all-to-all-start.1 = ((bf16[32,32,128]{2,1,0:T(8,128)(2,1)}), bf16[32,32,128]{2,1,0:T(8,128)(2,1)S(1)}, u32[]{:S(2)}, u32[]{:S(2)}) async-start(bf16[32,32,128]{2,1,0:T(8,128)(2,1)} %bitcast.42), calls=%async_computation.1 | async-start | bytes 524288 | tf_op jit(solution)/shard_map/all_to_all | solution.py:443
  202.0 9.3 %all-to-all-done.1 = bf16[32,32,128]{2,1,0:T(8,128)(2,1)S(1)} async-done(((bf16[32,32,128]{2,1,0:T(8,128)(2,1)}), bf16[32,32,128]{2,1,0:T(8,128)(2,1)S(1)}, u32[]{:S(2)}, u32[]{:S(2)}) %all-to-all-start.1) | async-done | bytes 262176 | tf_op jit(solution)/shard_map/all_to_all | solution.py:443
  211.3 3.5 %bpr_terms.1 = f32[512,1024]{1,0:T(8,128)} custom-call(s32[512,1]{1,0:T(8,128)S(1)} %copy.26.user_slot_ref, s32[512,1]{1,0:T(8,128)S(1)} %copy.27.item_slot_ref, bf16[1024,128]{1,0:T(8,128)(2,1)S(1)} %bitcast.58, bf16[1024,128]{1,0:T(8,128)(2,1)S(1)} %bitcast.60, bf16[1024,128]{1,0:T(8,128)(2,1)S(1)} %bitcast.59), custom_call_target="tpu_custom_call" | custom-call | tf_op jit(solution)/shard_map/bpr_terms/pallas_call | solution.py:258
  (119 shorter events, 38.2 us)
Async XLA Ops:
  2.3 16.1 %collective-permute-start.14 = (bf16[16,128,128]{2,1,0:T(8,128)(2,1)S(1)}, bf16[16,128,128]{2,1,0:T(8,128)(2,1)S(1)}, u32[]{:S(2)}, u32[]{:S(2)}) collective-permute-start(bf16[16,128,128]{2,1,0:T(8,128)(2,1)S(1)} %bitcast.54), channel_id=1, source_target_pairs={{0,2},{1,3},{2,4},{3,5},{4,6},{5,7},{8,10},{9,11},{10,12},{11,13},... | collective-permute-start | bytes 1572872 | tf_op jit(solution)/shard_map/ppermute | solution.py:304
  7.3 15.3 %collective-permute-start.15 = (bf16[16,128,128]{2,1,0:T(8,128)(2,1)S(1)}, bf16[16,128,128]{2,1,0:T(8,128)(2,1)S(1)}, u32[]{:S(2)}, u32[]{:S(2)}) collective-permute-start(bf16[16,128,128]{2,1,0:T(8,128)(2,1)S(1)} %bitcast.55), channel_id=1, source_target_pairs={{2,0},{3,1},{4,2},{5,3},{6,4},{7,5},{10,8},{11,9},{12,10},{13,11},... | collective-permute-start | bytes 1572872 | tf_op jit(solution)/shard_map/ppermute | solution.py:304
  8.6 69.9 %collective-permute-start.13 = (bf16[16,128,128]{2,1,0:T(8,128)(2,1)S(1)}, bf16[16,128,128]{2,1,0:T(8,128)(2,1)}, u32[]{:S(2)}, u32[]{:S(2)}) collective-permute-start(bf16[16,128,128]{2,1,0:T(8,128)(2,1)S(1)} %bitcast.56), channel_id=1, source_target_pairs={{0,1},{1,0},{2,3},{3,2},{4,5},{5,4},{6,7},{7,6},{8,9},{9,8},{10,11... | collective-permute-start | bytes 1572872 | tf_op jit(solution)/shard_map/ppermute | solution.py:304
  11.8 26.9 %collective-permute-start = (bf16[8,128,128]{2,1,0:T(8,128)(2,1)S(1)}, bf16[8,128,128]{2,1,0:T(8,128)(2,1)S(1)}, u32[]{:S(2)}, u32[]{:S(2)}) collective-permute-start(bf16[8,128,128]{2,1,0:T(8,128)(2,1)S(1)} %bitcast.68), channel_id=1, source_target_pairs={{0,8},{8,0},{16,24},{24,16},{1,9},{9,1},{17,25},{25,17},{2,10},{10... | collective-permute-start | bytes 786440 | tf_op jit(solution)/shard_map/ppermute | solution.py:307
  22.6 14.7 %collective-permute-start.18 = (bf16[16,128,128]{2,1,0:T(8,128)(2,1)S(1)}, bf16[16,128,128]{2,1,0:T(8,128)(2,1)}, u32[]{:S(2)}, u32[]{:S(2)}) collective-permute-start(bf16[16,128,128]{2,1,0:T(8,128)(2,1)S(1)} %collective-permute-done.15), channel_id=1, source_target_pairs={{2,0},{3,1},{4,2},{5,3},{10,8},{11,9},{12,10},{13,11},{18,16},{19,... | collective-permute-start | bytes 1572872 | tf_op jit(solution)/shard_map/ppermute | solution.py:304
  24.1 14.5 %collective-permute-start.2 = (bf16[8,128,128]{2,1,0:T(8,128)(2,1)S(1)}, bf16[8,128,128]{2,1,0:T(8,128)(2,1)}, u32[]{:S(2)}, u32[]{:S(2)}) collective-permute-start(bf16[8,128,128]{2,1,0:T(8,128)(2,1)S(1)} %collective-permute-done.1), channel_id=1, source_target_pairs={{0,8},{8,0},{16,24},{24,16},{1,9},{9,1},{17,25},{25,17},{2,10},{10... | collective-permute-start | bytes 786440 | tf_op jit(solution)/shard_map/ppermute | solution.py:307
  28.6 33.2 %collective-permute-start.20 = (bf16[16,128,128]{2,1,0:T(8,128)(2,1)S(1)}, bf16[16,128,128]{2,1,0:T(8,128)(2,1)S(1)}, u32[]{:S(2)}, u32[]{:S(2)}) collective-permute-start(bf16[16,128,128]{2,1,0:T(8,128)(2,1)S(1)} %collective-permute-done.17), channel_id=1, source_target_pairs={{4,6},{5,7},{12,14},{13,15},{20,22},{21,23},{28,30},{29,31}} | collective-permute-start | bytes 1572872 | tf_op jit(solution)/shard_map/ppermute | solution.py:304
  37.3 24.5 %collective-permute-start.21 = (bf16[16,128,128]{2,1,0:T(8,128)(2,1)}, bf16[16,128,128]{2,1,0:T(8,128)(2,1)S(1)}, u32[]{:S(2)}, u32[]{:S(2)}) collective-permute-start(bf16[16,128,128]{2,1,0:T(8,128)(2,1)} %collective-permute-done.18), channel_id=1, source_target_pairs={{2,0},{3,1},{10,8},{11,9},{18,16},{19,17},{26,24},{27,25}} | collective-permute-start | bytes 1572872 | tf_op jit(solution)/shard_map/ppermute | solution.py:304
  61.8 15.4 %collective-permute-start.5 = (bf16[16,128,128]{2,1,0:T(8,128)(2,1)}, bf16[16,128,128]{2,1,0:T(8,128)(2,1)}, u32[]{:S(2)}, u32[]{:S(2)}) collective-permute-start(bf16[16,128,128]{2,1,0:T(8,128)(2,1)} %get-tuple-element.24), channel_id=1, source_target_pairs={{0,1},{1,0},{2,3},{3,2},{4,5},{5,4},{6,7},{7,6},{8,9},{9,8},{10,11... | collective-permute-start | bytes 1572872 | tf_op jit(solution)/shard_map/ppermute | solution.py:304
  64.4 24.1 %collective-permute-start.16 = (bf16[16,128,128]{2,1,0:T(8,128)(2,1)S(1)}, bf16[16,128,128]{2,1,0:T(8,128)(2,1)}, u32[]{:S(2)}, u32[]{:S(2)}) collective-permute-start(bf16[16,128,128]{2,1,0:T(8,128)(2,1)S(1)} %get-tuple-element.43.rest_2_), channel_id=1, source_target_pairs={{0,1},{1,0},{2,3},{3,2},{4,5},{5,4},{6,7},{7,6},{8,9},{9,8},{10,11... | collective-permute-start | bytes 1572872 | tf_op jit(solution)/shard_map/ppermute | solution.py:304
  66.7 90.2 %all-to-all-start = ((s32[32,2,32]{2,1,0:T(2,128)}), s32[32,2,32]{2,1,0:T(2,128)S(1)}, u32[]{:S(2)}, u32[]{:S(2)}) async-start(s32[32,2,32]{2,1,0:T(2,128)} %pad_add_fusion), calls=%async_computation | async-start | bytes 65536 | tf_op jit(solution)/shard_map/all_to_all | solution.py:425
  72.3 72.2 %collective-permute-start.6 = (bf16[16,128,128]{2,1,0:T(8,128)(2,1)}, bf16[16,128,128]{2,1,0:T(8,128)(2,1)S(1)}, u32[]{:S(2)}, u32[]{:S(2)}) collective-permute-start(bf16[16,128,128]{2,1,0:T(8,128)(2,1)} %copy-done.12), channel_id=1, source_target_pairs={{0,1},{1,0},{2,3},{3,2},{4,5},{5,4},{6,7},{7,6},{8,9},{9,8},{10,11... | collective-permute-start | bytes 1572872 | tf_op jit(solution)/shard_map/ppermute | solution.py:304
  74.0 36.9 %collective-permute-start.19 = (bf16[16,128,128]{2,1,0:T(8,128)(2,1)S(1)}, bf16[16,128,128]{2,1,0:T(8,128)(2,1)S(1)}, u32[]{:S(2)}, u32[]{:S(2)}) collective-permute-start(bf16[16,128,128]{2,1,0:T(8,128)(2,1)S(1)} %get-tuple-element.40.rest_4_), channel_id=1, source_target_pairs={{0,1},{1,0},{2,3},{3,2},{4,5},{5,4},{6,7},{7,6},{8,9},{9,8},{10,11... | collective-permute-start | bytes 1572872 | tf_op jit(solution)/shard_map/ppermute | solution.py:304
  77.1 45.1 %collective-permute-start.22 = (bf16[16,128,128]{2,1,0:T(8,128)(2,1)S(1)}, bf16[16,128,128]{2,1,0:T(8,128)(2,1)S(1)}, u32[]{:S(2)}, u32[]{:S(2)}) collective-permute-start(bf16[16,128,128]{2,1,0:T(8,128)(2,1)S(1)} %get-tuple-element.39.rest_6_), channel_id=1, source_target_pairs={{0,1},{1,0},{2,3},{3,2},{4,5},{5,4},{6,7},{7,6},{8,9},{9,8},{10,11... | collective-permute-start | bytes 1572872 | tf_op jit(solution)/shard_map/ppermute | solution.py:304
  78.5 66.0 %collective-permute-start.10 = (bf16[16,128,128]{2,1,0:T(8,128)(2,1)S(1)}, bf16[16,128,128]{2,1,0:T(8,128)(2,1)S(1)}, u32[]{:S(2)}, u32[]{:S(2)}) collective-permute-start(bf16[16,128,128]{2,1,0:T(8,128)(2,1)S(1)} %add_convert_fusion.5), channel_id=1, source_target_pairs={{6,4},{7,5},{14,12},{15,13},{22,20},{23,21},{30,28},{31,29}} | collective-permute-start | bytes 1572872 | tf_op jit(solution)/shard_map/ppermute | solution.py:304
  88.5 56.0 %collective-permute-start.7 = (bf16[16,128,128]{2,1,0:T(8,128)(2,1)S(1)}, bf16[16,128,128]{2,1,0:T(8,128)(2,1)S(1)}, u32[]{:S(2)}, u32[]{:S(2)}) collective-permute-start(bf16[16,128,128]{2,1,0:T(8,128)(2,1)S(1)} %add_convert_fusion.5), channel_id=1, source_target_pairs={{0,2},{1,3},{8,10},{9,11},{16,18},{17,19},{24,26},{25,27}} | collective-permute-start | bytes 1572872 | tf_op jit(solution)/shard_map/ppermute | solution.py:304
  110.9 59.2 %collective-permute-start.4 = (bf16[16,128,128]{2,1,0:T(8,128)(2,1)}, bf16[16,128,128]{2,1,0:T(8,128)(2,1)}, u32[]{:S(2)}, u32[]{:S(2)}) collective-permute-start(bf16[16,128,128]{2,1,0:T(8,128)(2,1)} %copy-done.11), channel_id=1, source_target_pairs={{0,1},{1,0},{2,3},{3,2},{4,5},{5,4},{6,7},{7,6},{8,9},{9,8},{10,11... | collective-permute-start | bytes 1572872 | tf_op jit(solution)/shard_map/ppermute | solution.py:304
  146.0 24.2 %collective-permute-start.11 = (bf16[16,128,128]{2,1,0:T(8,128)(2,1)}, bf16[16,128,128]{2,1,0:T(8,128)(2,1)}, u32[]{:S(2)}, u32[]{:S(2)}) collective-permute-start(bf16[16,128,128]{2,1,0:T(8,128)(2,1)} %get-tuple-element.37), channel_id=1, source_target_pairs={{4,2},{5,3},{6,4},{7,5},{12,10},{13,11},{14,12},{15,13},{20,18},{2... | collective-permute-start | bytes 1572872 | tf_op jit(solution)/shard_map/ppermute | solution.py:304
  147.4 22.8 %collective-permute-start.8 = (bf16[16,128,128]{2,1,0:T(8,128)(2,1)}, bf16[16,128,128]{2,1,0:T(8,128)(2,1)}, u32[]{:S(2)}, u32[]{:S(2)}) collective-permute-start(bf16[16,128,128]{2,1,0:T(8,128)(2,1)} %get-tuple-element.38), channel_id=1, source_target_pairs={{0,2},{1,3},{2,4},{3,5},{8,10},{9,11},{10,12},{11,13},{16,18},{17,... | collective-permute-start | bytes 1572872 | tf_op jit(solution)/shard_map/ppermute | solution.py:304
  164.8 30.6 %all-to-all-start.2 = ((bf16[32,64,128]{2,1,0:T(8,128)(2,1)}), bf16[32,64,128]{2,1,0:T(8,128)(2,1)}, u32[]{:S(2)}, u32[]{:S(2)}) async-start(bf16[32,64,128]{2,1,0:T(8,128)(2,1)} %pad_maximum_fusion.1), calls=%async_computation.2 | async-start | bytes 1048576 | tf_op jit(solution)/shard_map/all_to_all | solution.py:436
  168.4 19.6 %collective-permute-start.3 = (bf16[16,128,128]{2,1,0:T(8,128)(2,1)}, bf16[16,128,128]{2,1,0:T(8,128)(2,1)S(1)}, u32[]{:S(2)}, u32[]{:S(2)}) collective-permute-start(bf16[16,128,128]{2,1,0:T(8,128)(2,1)} %get-tuple-element.20), channel_id=1, source_target_pairs={{0,1},{1,0},{2,3},{3,2},{4,5},{5,4},{6,7},{7,6},{8,9},{9,8},{10,11... | collective-permute-start | bytes 1572872 | tf_op jit(solution)/shard_map/ppermute | solution.py:304
  173.4 18.8 %collective-permute-start.12 = (bf16[16,128,128]{2,1,0:T(8,128)(2,1)}, bf16[16,128,128]{2,1,0:T(8,128)(2,1)S(1)}, u32[]{:S(2)}, u32[]{:S(2)}) collective-permute-start(bf16[16,128,128]{2,1,0:T(8,128)(2,1)} %get-tuple-element.41), channel_id=1, source_target_pairs={{2,0},{3,1},{4,2},{5,3},{6,4},{7,5},{10,8},{11,9},{12,10},{13,11},... | collective-permute-start | bytes 1572872 | tf_op jit(solution)/shard_map/ppermute | solution.py:304
  174.7 17.5 %collective-permute-start.9 = (bf16[16,128,128]{2,1,0:T(8,128)(2,1)}, bf16[16,128,128]{2,1,0:T(8,128)(2,1)}, u32[]{:S(2)}, u32[]{:S(2)}) collective-permute-start(bf16[16,128,128]{2,1,0:T(8,128)(2,1)} %get-tuple-element.42), channel_id=1, source_target_pairs={{0,2},{1,3},{2,4},{3,5},{4,6},{5,7},{8,10},{9,11},{10,12},{11,13},... | collective-permute-start | bytes 1572872 | tf_op jit(solution)/shard_map/ppermute | solution.py:304
  195.4 15.8 %all-to-all-start.1 = ((bf16[32,32,128]{2,1,0:T(8,128)(2,1)}), bf16[32,32,128]{2,1,0:T(8,128)(2,1)S(1)}, u32[]{:S(2)}, u32[]{:S(2)}) async-start(bf16[32,32,128]{2,1,0:T(8,128)(2,1)} %bitcast.42), calls=%async_computation.1 | async-start | bytes 524288 | tf_op jit(solution)/shard_map/all_to_all | solution.py:443
  (25 other events, 352.1 us)

commit v2 on v0

v2 whole, which is shorter than its diff:
```python
import functools

import jax
import jax.numpy as jnp
import numpy as np
from jax import lax
from jax.experimental import pallas as pl
from jax.experimental.pallas import tpu as pltpu
from jax.sharding import PartitionSpec as P

F32 = jnp.float32
BF16 = jnp.bfloat16
VMEM_WHOLE = pl.BlockSpec(memory_space=pltpu.VMEM)


def split_axis(size):
    fast = max(d for d in range(1, size + 1) if size % d == 0 and d * d <= size)
    return size // fast, fast


def ring_of(size):
    slow, fast = split_axis(size)
    walk = [(a, 0) for a in range(slow)]
    for turn, a in enumerate(reversed(range(slow))):
        across = range(1, fast)
        walk += [(a, b) for b in (across if turn % 2 == 0 else reversed(across))]
    return [a * fast + b for a, b in walk]


def group_of(slots):
    return next(g for g in (64, 32, 16, 8, 4, 2, 1) if slots % g == 0)


def add_tiles(count, vals_hbm, held, sems, left, right, place, trash, total, before):
    most = sems.shape[0]
    group = held.shape[0] // most
    groups = (count + group - 1) // group

    def fetch(number):
        some = pl.ds(number * group, group)
        return pltpu.make_async_copy(vals_hbm.at[some], held.at[some], sems.at[number])

    def fetch_all(numbers):
        for number in numbers:

            @pl.when(number < groups)
            def _(number=number):
                fetch(number).start()

    fetch_all(range(1))
    total[...] = jnp.zeros_like(total)
    for copy in before:
        copy.wait()
    fetch_all(range(1, most))

    def one_group(number, carry):
        fetch(number).wait()
        products, places = [], []
        for u in range(group):
            slot = number * group + u
            products.append(jnp.dot(left(slot), right(slot), preferred_element_type=F32))
            places.append(jnp.where(slot < count, place(slot), trash))
        for product, at in zip(products, places):
            total[at] += product
        return carry

    lax.fori_loop(0, groups, one_group, 0)


def hand_out(total, bases, outs):
    for n, out in enumerate(outs):

        def tile(i, carry, n=n, out=out):
            out[i] = total[bases[n] + i].astype(BF16)
            return carry

        lax.fori_loop(0, out.shape[0], tile, 0, unroll=min(8, out.shape[0]))


def fill(table, bases, blocks, sems):
    copies = [
        pltpu.make_async_copy(block, table.at[pl.ds(base, block.shape[0])], sems.at[n])
        for n, (base, block) in enumerate(zip(bases, blocks))
    ]
    for copy in copies:
        copy.start()
    return copies


def term_kernel(count_ref, rows_ref, cols_ref, in_ref, out_ref, vals_ref, *rest, axes, blocks, trash, to_users):
    given = rest[:blocks]
    *outs, held, table, total, sems, table_sems = rest[blocks:]
    place_in, place_out = lax.axis_index(axes[0]), lax.axis_index(axes[1])
    copies = fill(table, [in_ref[place_in, n] for n in range(blocks)], given, table_sems)
    places_ref, others_ref = (rows_ref, cols_ref) if to_users else (cols_ref, rows_ref)

    def values(slot):
        return held[slot]

    def other(slot):
        return table[others_ref[slot]]

    left, right = (values, other) if to_users else (other, values)
    add_tiles(
        count_ref[0], vals_ref, held, sems, left, right, lambda slot: places_ref[slot], trash, total, copies
    )
    hand_out(total, [out_ref[place_out, n] for n in range(len(outs))], outs)


SMEM_WHOLE = pl.BlockSpec(memory_space=pltpu.SMEM)
TERM_VMEM = 52 * 2**20
HBM_WHOLE = pl.BlockSpec(memory_space=pltpu.HBM)


def tile_cost(vals, embed):
    slots, side = vals.shape[0], vals.shape[1]
    return pl.CostEstimate(
        flops=2 * slots * side * side * embed, bytes_accessed=2 * slots * side * side, transcendentals=0
    )


def terms(count, rows, cols, in_table, out_table, vals, blocks, axes, tiles, to_users):
    slots, side = vals.shape[0], vals.shape[1]
    group = group_of(slots)
    table = sum(block.shape[0] for block in blocks)
    tile = blocks[0].shape[1:]
    outs = out_table.shape[1]
    return pl.pallas_call(
        functools.partial(
            term_kernel, axes=axes, blocks=len(blocks), trash=tiles, to_users=to_users
        ),
        in_specs=[SMEM_WHOLE] * 5 + [HBM_WHOLE] + [pl.BlockSpec(memory_space=pl.ANY)] * len(blocks),
        out_specs=[VMEM_WHOLE] * outs,
        scratch_shapes=[
            pltpu.VMEM(vals.shape, BF16),
            pltpu.VMEM((table, *tile), BF16),
            pltpu.VMEM((tiles + 1, *tile), F32),
            pltpu.SemaphoreType.DMA((slots // group,)),
            pltpu.SemaphoreType.DMA((len(blocks),)),
        ],
        out_shape=[jax.ShapeDtypeStruct((tiles // outs, *tile), BF16) for _ in range(outs)],
        compiler_params=pltpu.CompilerParams(vmem_limit_bytes=TERM_VMEM),
        cost_estimate=tile_cost(vals, tile[1]),
        name="user_terms" if to_users else "item_terms",
    )(count, rows, cols, in_table, out_table, vals, *blocks)


def picked_rows(wanted_ref, low, out_ref, chunk):
    rows = low.shape[0]
    for at in range(0, wanted_ref.shape[0], chunk):
        some = min(chunk, wanted_ref.shape[0] - at)
        hot = wanted_ref[pl.ds(at, some), :] == lax.broadcasted_iota(jnp.int32, (some, rows), 1)
        out_ref[pl.ds(at, some), :] = jnp.dot(hot.astype(BF16), low, preferred_element_type=F32).astype(BF16)


def combine_kernel(emb_ref, wanted_ref, *rest, terms, transposed):
    parts = rest[:terms]
    final_ref, rows_ref = rest[terms:]
    side = parts[0].shape[-2]
    for i in range(parts[0].shape[0]):
        at = pl.ds(i * side, side)
        prop = functools.reduce(jnp.add, [part[i].astype(F32) for part in parts])
        if transposed:
            prop = prop.T
        final_ref[at, :] = (emb_ref[at, :] + prop) * 0.5
    picked_rows(wanted_ref, final_ref[...].astype(BF16), rows_ref, 256)


def combine(emb, parts, wanted, transposed, name):
    return pl.pallas_call(
        functools.partial(combine_kernel, terms=len(parts), transposed=transposed),
        in_specs=[VMEM_WHOLE] * (2 + len(parts)),
        out_specs=[VMEM_WHOLE] * 2,
        out_shape=[
            jax.ShapeDtypeStruct(emb.shape, F32),
            jax.ShapeDtypeStruct((wanted.shape[0], emb.shape[1]), BF16),
        ],
        compiler_params=pltpu.CompilerParams(vmem_limit_bytes=32 * 2**20),
        name=name,
    )(emb, wanted, *parts)


def bpr_kernel(user_slot_ref, item_slot_ref, users_ref, items_ref, negatives_ref, out_ref):
    def vectors(slot_ref, rows_ref):
        hot = slot_ref[...] == lax.broadcasted_iota(jnp.int32, (slot_ref.shape[0], rows_ref.shape[0]), 1)
        return jnp.dot(hot.astype(BF16), rows_ref[...], preferred_element_type=F32)

    users = vectors(user_slot_ref, users_ref)
    items = vectors(item_slot_ref, items_ref)
    positive = jnp.sum(users * items, axis=1, keepdims=True)
    against = lax.dot_general(
        users.astype(BF16), negatives_ref[...], (((1,), (1,)), ((), ())), preferred_element_type=F32
    )
    out_ref[...] = jnp.log1p(jnp.exp(against - positive))


def bpr(user_slot, item_slot, users, items, negatives):
    pairs, embed = user_slot.shape[0], users.shape[1]
    block = next(b for b in (128, 64, 32, 16, 8, pairs) if pairs % b == 0)
    whole = lambda array: pl.BlockSpec(array.shape, lambda i: (0, 0))
    return pl.pallas_call(
        bpr_kernel,
        grid=(pairs // block,),
        in_specs=[pl.BlockSpec((block, 1), lambda i: (i, 0))] * 2 + [whole(users), whole(items), whole(negatives)],
        out_specs=pl.BlockSpec((block, negatives.shape[0]), lambda i: (i, 0)),
        out_shape=jax.ShapeDtypeStruct((pairs, negatives.shape[0]), F32),
        compiler_params=pltpu.CompilerParams(
            dimension_semantics=("arbitrary",), vmem_limit_bytes=32 * 2**20
        ),
        name="bpr_terms",
    )(user_slot, item_slot, users, items, negatives)


def place_requests(owner, local, slots):
    pairs = owner.shape[0]
    order = jnp.arange(pairs, dtype=jnp.int32)
    same = (owner[:, None] == owner[None, :]) & (order[None, :] < order[:, None])
    slot = owner * slots + jnp.sum(same.astype(jnp.int32), axis=1)
    return slot


def requests_of(slot, local, total):
    hits = slot[:, None] == jnp.arange(total, dtype=jnp.int32)[None, :]
    return jnp.sum(jnp.where(hits, local[:, None], 0), axis=0)


def on_device(user_emb, item_emb, tile_vals, tile_rows, tile_cols, tile_count, pair_users, pair_items, negatives):
    row_count, col_count = lax.axis_size("row"), lax.axis_size("col")
    row, col = lax.axis_index("row"), lax.axis_index("col")
    devices = row_count * col_count
    user_dev, embed = user_emb.shape[2:]
    item_dev = item_emb.shape[2]
    side = tile_vals.shape[-1]
    user_tiles, item_tiles = user_dev // side, item_dev // side
    ring = ring_of(col_count)

    def ring_table(shifts):
        places = [[ring[(ring.index(c) + shift) % col_count] for shift in shifts] for c in range(col_count)]
        return np.asarray(places, np.int32) * user_tiles

    def around(array, shift):
        pairs = [(ring[p], ring[(p + shift) % col_count]) for p in range(col_count)]
        return lax.ppermute(array, "col", pairs)

    row_slow, row_fast = (row_count, 1) if row_count % 2 else (row_count // 2, 2)

    def row_table(steps):
        places = [
            [(r // row_fast + j) % row_slow * row_fast + (r + i) % row_fast for j, i in steps] for r in range(row_count)
        ]
        return np.asarray(places, np.int32) * item_tiles

    user_mine, item_mine = user_emb[0, 0], item_emb[0, 0]
    count, rows, cols = tile_count[0], tile_rows[0, 0], tile_cols[0, 0]
    vals = tile_vals[0, 0]
    user_low = jnp.swapaxes(user_mine.astype(BF16).reshape(user_tiles, side, embed), 1, 2)
    item_low = item_mine.astype(BF16).reshape(item_tiles, side, embed)

    def send_row(array, step):
        pairs = [
            (a * row_fast + b, step(a, b)[0] * row_fast + step(a, b)[1])
            for a in range(row_slow)
            for b in range(row_fast)
        ]
        return lax.ppermute(array, "row", pairs)

    halves = [item_low]
    for j in range(1, row_slow):
        halves.append(send_row(item_low, lambda a, b, j=j: ((a + j) % row_slow, b)))
    item_blocks = list(halves)
    item_steps = [(-j, 0) for j in range(row_slow)]
    for i in range(1, row_fast):
        for j, half in enumerate(halves):
            item_blocks.append(send_row(half, lambda a, b, i=i: (a, (b + i) % row_fast)))
            item_steps.append((-j, -i))

    slots = 2 * pair_users.shape[0] // devices
    user_owner, user_local = pair_users // user_dev, pair_users % user_dev
    item_holder, item_local = pair_items // item_dev, pair_items % item_dev
    item_owner = item_holder % row_count * col_count + item_holder // row_count
    user_slot = place_requests(user_owner, user_local, slots)
    item_slot = place_requests(item_owner, item_local, slots)
    asked = jnp.stack(
        [
            requests_of(user_slot, user_local, devices * slots).reshape(devices, slots),
            requests_of(item_slot, item_local, devices * slots).reshape(devices, slots),
        ],
        axis=1,
    )
    neg_each = negatives.shape[0] // devices
    offset = (col * row_count + row) * item_dev
    named = lax.dynamic_slice_in_dim(negatives, (row * col_count + col) * neg_each, neg_each, 0) - offset

    right, left = (col_count - 1) // 2, col_count // 2
    shifts = [0]
    for s in range(1, left + 1):
        shifts += [s] + ([-s] if s <= right else [])
    user_blocks = [(user_low, 0)]
    from_left = from_right = user_low
    part = None
    for s in range(1, left + 1):
        if s <= right:
            from_left = around(from_left, 1)
            user_blocks.append((from_left, -s))
        from_right = around(from_right, -1)
        user_blocks.append((from_right, s))
        if s == 1:
            tied = lax.optimization_barrier((item_blocks, from_left, from_right))
            user_parts = terms(
                count,
                rows,
                cols,
                row_table(item_steps),
                ring_table(shifts),
                vals,
                tied[0],
                ("row", "col"),
                col_count * user_tiles,
                True,
            )
            part = dict(zip(shifts, user_parts))
        if s == 2:
            from_left, from_right, part[0] = lax.optimization_barrier((from_left, from_right, part[0]))

    asked, part[0] = lax.optimization_barrier((asked, part[0]))
    wanted = lax.all_to_all(asked, ("row", "col"), split_axis=0, concat_axis=0, tiled=True)

    def plus(mine, more):
        return mine if more is None else (mine.astype(F32) + more.astype(F32)).astype(BF16)

    to_right = to_left = None
    for s in range(left, 0, -1):
        to_right = around(plus(part[s], to_right), 1)
        if s <= right:
            to_left = around(plus(part[-s], to_left), -1)
    user_terms_in = [part[0]] + [more for more in (to_right, to_left) if more is not None]

    out_steps = [(j, i) for j in range(row_slow) for i in range(row_fast)]
    item_out = terms(
        count,
        rows,
        cols,
        ring_table([shift for _, shift in user_blocks]),
        row_table(out_steps),
        vals,
        [block for block, _ in user_blocks],
        ("col", "row"),
        row_count * item_tiles,
        False,
    )
    item_sums = []
    for j in range(row_slow):
        mine = [item_out[j * row_fast]] + [
            send_row(item_out[j * row_fast + i], lambda a, b, i=i: (a, (b + i) % row_fast))
            for i in range(1, row_fast)
        ]
        if j:
            total = functools.reduce(jnp.add, [part.astype(F32) for part in mine]).astype(BF16)
            item_sums.append(send_row(total, lambda a, b, j=j: ((a + j) % row_slow, b)))
        else:
            item_sums += mine

    user_wanted = wanted[:, 0].reshape(-1, 1)
    item_wanted = jnp.concatenate([wanted[:, 1].reshape(-1), named]).reshape(-1, 1)

    item_final, item_rows = combine(item_mine, item_sums, item_wanted, True, "item_final")
    asked_rows = item_rows[: devices * slots].reshape(devices, slots, embed)
    named_rows = jnp.broadcast_to(item_rows[None, devices * slots :], (devices, neg_each, embed))
    item_back = lax.all_to_all(
        jnp.concatenate([asked_rows, named_rows], axis=1), ("row", "col"), split_axis=0, concat_axis=0, tiled=True
    )
    item_table_back = item_back[:, :slots].reshape(devices * slots, embed)
    negative_rows = item_back[:, slots:].reshape(devices * neg_each, embed)

    user_final, user_rows = combine(user_mine, user_terms_in, user_wanted, False, "user_final")
    user_back = lax.all_to_all(
        user_rows.reshape(devices, slots, embed), ("row", "col"), split_axis=0, concat_axis=0, tiled=True
    ).reshape(devices * slots, embed)
    bpr_terms = bpr(user_slot[:, None], item_slot[:, None], user_back, item_table_back, negative_rows)
    return user_final.reshape(user_emb.shape), item_final.reshape(item_emb.shape), bpr_terms


def solution(mesh):
    placed = (
        P("row", "col", None, None),
        P("col", "row", None, None),
        P("row", "col", None, None, None),
        P("row", "col", None),
        P("row", "col", None),
        P("row", "col"),
        P(("row", "col")),
        P(("row", "col")),
        P(),
    )
    return jax.shard_map(
        on_device,
        mesh=mesh,
        in_specs=placed,
        out_specs=(
            P("row", "col", None, None),
            P("col", "row", None, None),
            P(("row", "col"), None),
        ),
        check_vma=False,
    )
```

time: 656 us -> 134 us (0.20)
  starting transfers between devices: 176 us -> 37.1 us
  waiting for transfers between devices: 182 us -> 53.2 us
  other arithmetic: 113 us -> 12.5 us
  blocking collectives: 71.9 us -> 0 us
  local copies, waits for them, and re-layouts: 51 us -> 4.48 us
  matrix products: 43.5 us -> 0 us
  Pallas kernels: 0 us -> 23.9 us
  between operations: 14.7 us -> 1.73 us
    all_to_all x4 -> x3, starting transfers between devices: 176 us -> 15.6 us  [the longest x1 6.46 us: on_device(): lax.all_to_all(user_rows.reshape(devices, slots, embed), ('row', 'col'),...]
    all_gather x2 -> x0, waiting for transfers between devices: 93.8 us -> none  [the longest x1 76.1 us: on_device(): lax.all_gather(user_emb.astype(jnp.bfloat16), 'col', axis=1, tiled=True)]
    scatter-add x8 -> x0, other arithmetic: 89.6 us -> none  [the longest x4 54.4 us: advance(): user_part.at[row_ids].add(to_users)]
    reduce_scatter x2 -> x0, waiting for transfers between devices: 79.7 us -> none  [the longest x1 79.7 us: on_device(): lax.psum_scatter(user_part.reshape(-1, embed).astype(jnp.bfloat16), 'col'...]
    all_gather x1 -> x0, blocking collectives: 71.9 us -> none  [on_device(): lax.all_gather(item_final[mine], ('row', 'col'), axis=0, tiled=True)]
    ppermute x0 -> x20, waiting for transfers between devices: none -> 44 us  [the longest x14 32.7 us: around(): return lax.ppermute(array, 'col', pairs)]
    dot_general x9 -> x0, matrix products: 43.5 us -> none  [the longest x4 20.9 us: advance(): jnp.einsum('tij,tie->tje', values, user_tiles[row_ids], preferred_element...]
    gather x14 -> x0, local copies, waits for them, and re-layouts: 37.9 us -> none  [the longest x4 17.3 us: advance(): user_tiles[row_ids]]
  transfers between devices with their start and end apart: 8 -> 23, of which waited for: 5 -> 10; matrix products, arithmetic and copies ran while one was open for 5% -> 10% of each run, Pallas kernels for 0% -> 15%
where the time goes in v2:
time: 134 us; the launch traced here: 133 us
  waiting for transfers between devices  53.2 us (40%)
  starting transfers between devices  37.1 us (28%)
  Pallas kernels  23.9 us (18%)
  other arithmetic  12.5 us (9%)
  local copies, waits for them, and re-layouts  4.48 us (3%)
  between operations  1.73 us (1%)
    ppermute x14, waiting for transfers between devices, around(): return lax.ppermute(array, 'col', pairs)  32.7 us
    ppermute x14, starting transfers between devices, around(): return lax.ppermute(array, 'col', pairs)  17.6 us
    pallas_call x2, Pallas kernels, terms(): pl.pallas_call(functools.partial(term_kernel, axes=axes, blocks=len(block...  17.2 us
    ppermute x6, waiting for transfers between devices, send_row(): return lax.ppermute(array, 'row', pairs)  11.2 us
    all_to_all x1, waiting for transfers between devices, on_device(): lax.all_to_all(user_rows.reshape(devices, slots, embed), ('row', 'col'),...  9.26 us
    convert_element_type x5, other arithmetic, plus(): (mine.astype(F32) + more.astype(F32)).astype(BF16)  7.67 us
    all_to_all x1, starting transfers between devices, on_device(): lax.all_to_all(user_rows.reshape(devices, slots, embed), ('row', 'col'),...  6.46 us
    all_to_all x1, starting transfers between devices, on_device(): lax.all_to_all(asked, ('row', 'col'), split_axis=0, concat_axis=0, tiled=...  4.91 us
  transfers between devices with their start and end apart: 23, of which 10 were waited for; matrix products, arithmetic and copies ran while one was open for 10% of the time, Pallas kernels for 15%

profile of v2, /device:TPU:0, one launch (start us, length us, event | category | flops | bytes accessed | tf_op | source)
XLA Modules:
  0.0 132.9 jit_solution(13030225564654869410)
XLA Ops:
  2.3 3.1 %collective-permute-start = (bf16[16,128,128]{2,1,0:T(8,128)(2,1)S(1)}, bf16[16,128,128]{2,1,0:T(8,128)(2,1)S(1)}, u32[]{:S(2)}, u32[]{:S(2)}) collective-permute-start(bf16[16,128,128]{2,1,0:T(8,128)(2,1)S(1)} %bitcast.22), channel_id=1, source_target_pairs={{0,2},{2,4},{4,6},{6,7},{7,5},{5,3},{3,1},{1,0},{8,10},{10,12},{12... | collective-permute-start | bytes 1572872 | tf_op jit(solution)/shard_map/ppermute | solution.py:243
  5.5 2.0 %collective-permute-start.4 = (bf16[8,128,128]{2,1,0:T(8,128)(2,1)S(1)}, bf16[8,128,128]{2,1,0:T(8,128)(2,1)S(1)}, u32[]{:S(2)}, u32[]{:S(2)}) collective-permute-start(bf16[8,128,128]{2,1,0:T(8,128)(2,1)S(1)} %bitcast.25), channel_id=1, source_target_pairs={{0,16},{8,24},{16,0},{24,8},{1,17},{9,25},{17,1},{25,9},{2,18},{10... | collective-permute-start | bytes 786440 | tf_op jit(solution)/shard_map/ppermute | solution.py:265
  7.8 5.5 %collective-permute-done.4.rest_1_ = bf16[8,128,128]{2,1,0:T(8,128)(2,1)S(1)} collective-permute-done((bf16[8,128,128]{2,1,0:T(8,128)(2,1)S(1)}, bf16[8,128,128]{2,1,0:T(8,128)(2,1)S(1)}, u32[]{:S(2)}, u32[]{:S(2)}) %collective-permute-start.4) | collective-permute-done | bytes 262176 | tf_op jit(solution)/shard_map/ppermute | solution.py:265
  13.3 4.0 %collective-permute-done.rest_1_ = bf16[16,128,128]{2,1,0:T(8,128)(2,1)S(1)} collective-permute-done((bf16[16,128,128]{2,1,0:T(8,128)(2,1)S(1)}, bf16[16,128,128]{2,1,0:T(8,128)(2,1)S(1)}, u32[]{:S(2)}, u32[]{:S(2)}) %collective-permute-start) | collective-permute-done | bytes 524320 | tf_op jit(solution)/shard_map/ppermute | solution.py:243
  17.3 1.8 %collective-permute-start.1 = (bf16[16,128,128]{2,1,0:T(8,128)(2,1)S(1)}, bf16[16,128,128]{2,1,0:T(8,128)(2,1)}, u32[]{:S(2)}, u32[]{:S(2)}) collective-permute-start(bf16[16,128,128]{2,1,0:T(8,128)(2,1)S(1)} %collective-permute-done.rest_1_), channel_id=1, source_target_pairs={{0,2},{2,4},{4,6},{6,7},{7,5},{5,3},{3,1},{1,0},{8,10},{10,12},{12... | collective-permute-start | bytes 1572872 | tf_op jit(solution)/shard_map/ppermute | solution.py:243
  20.1 9.1 %user_terms.1 = (bf16[16,128,128]{2,1,0:T(8,128)(2,1)S(1)}, bf16[16,128,128]{2,1,0:T(8,128)(2,1)}, bf16[16,128,128]{2,1,0:T(8,128)(2,1)}, bf16[16,128,128]{2,1,0...) custom-call(s32[1]{0:T(128)} %bitcast.18.count_ref, ...), custom_call_target="tpu_custom_call" | custom-call | flops 2147483648 | bytes 16777216 | tf_op jit(solution)/shard_map/user_terms/pallas_call | solution.py:128
  35.0 1.6 %collective-permute-start.14 = (bf16[16,128,128]{2,1,0:T(8,128)(2,1)}, bf16[16,128,128]{2,1,0:T(8,128)(2,1)S(1)}, u32[]{:S(2)}, u32[]{:S(2)}) collective-permute-start(bf16[16,128,128]{2,1,0:T(8,128)(2,1)} %collective-permute-done.1.rest_3_), channel_id=1, source_target_pairs={{0,2},{2,4},{4,6},{6,7},{7,5},{5,3},{3,1},{1,0},{8,10},{10,12},{12... | collective-permute-start | bytes 1572872 | tf_op jit(solution)/shard_map/ppermute | solution.py:243
  36.7 7.7 %collective-permute-done.15.rest_6_ = bf16[16,128,128]{2,1,0:T(8,128)(2,1)S(1)} collective-permute-done((bf16[16,128,128]{2,1,0:T(8,128)(2,1)S(1)}, bf16[16,128,128]{2,1,0:T(8,128)(2,1)S(1)}, u32[]{:S(2)}, u32[]{:S(2)}) %collective-permute-start.15) | collective-permute-done | bytes 524320 | tf_op jit(solution)/shard_map/ppermute | solution.py:243
  48.2 4.9 %all-to-all-start = ((s32[32,2,32]{2,1,0:T(2,128)}), s32[32,2,32]{2,1,0:T(2,128)S(1)}, u32[]{:S(2)}, u32[]{:S(2)}) async-start(s32[32,2,32]{2,1,0:T(2,128)} %pad_add_fusion), calls=%async_computation | async-start | bytes 65536 | tf_op jit(solution)/shard_map/all_to_all | solution.py:326
  54.5 1.8 %collective-permute-start.8 = (bf16[16,128,128]{2,1,0:T(8,128)(2,1)S(1)}, bf16[16,128,128]{2,1,0:T(8,128)(2,1)S(1)}, u32[]{:S(2)}, u32[]{:S(2)}) collective-permute-start(bf16[16,128,128]{2,1,0:T(8,128)(2,1)S(1)} %add_convert_fusion.4), channel_id=1, source_target_pairs={{0,2},{2,4},{4,6},{6,7},{7,5},{5,3},{3,1},{1,0},{8,10},{10,12},{12... | collective-permute-start | bytes 1572872 | tf_op jit(solution)/shard_map/ppermute | solution.py:243
  57.2 2.0 %collective-permute-done.16.rest_7_ = bf16[16,128,128]{2,1,0:T(8,128)(2,1)S(1)} collective-permute-done((bf16[16,128,128]{2,1,0:T(8,128)(2,1)S(1)}, bf16[16,128,128]{2,1,0:T(8,128)(2,1)S(1)}, u32[]{:S(2)}, u32[]{:S(2)}) %collective-permute-start.16) | collective-permute-done | bytes 524320 | tf_op jit(solution)/shard_map/ppermute | solution.py:243
  60.1 8.1 %item_terms.1 = (bf16[8,128,128]{2,1,0:T(8,128)(2,1)S(1)}, bf16[8,128,128]{2,1,0:T(8,128)(2,1)S(1)}, bf16[8,128,128]{2,1,0:T(8,128)(2,1)S(1)}, bf16[8,128,128]{2,1,0:T(8,128)(2,1)S(1)}) custom-call(s32[1]{0:T(128)} %bitcast.19.count_ref, s32[512]{0:T(512)S(1)} %bitcast.32, s32[512]{0:T(512)S(1)} %bitcast.34, s32[8,8]{1,0:T(8,128)S(1)} %copy-done.4, ...), custom_call_target="tpu_custom_call" | custom-call | flops 2147483648 | bytes 16777216 | tf_op jit(solution)/shard_map/item_terms/pallas_call | solution.py:128
  69.6 3.0 %collective-permute-start.12 = (bf16[16,128,128]{2,1,0:T(8,128)(2,1)S(1)}, bf16[16,128,128]{2,1,0:T(8,128)(2,1)}, u32[]{:S(2)}, u32[]{:S(2)}) collective-permute-start(bf16[16,128,128]{2,1,0:T(8,128)(2,1)S(1)} %add_convert_fusion.1), channel_id=1, source_target_pairs={{0,1},{2,0},{4,2},{6,4},{7,6},{5,7},{3,5},{1,3},{8,9},{10,8},{12,1... | collective-permute-start | bytes 1572872 | tf_op jit(solution)/shard_map/ppermute | solution.py:243
  72.8 1.6 %collective-permute-start.19 = (bf16[8,128,128]{2,1,0:T(8,128)(2,1)S(1)}, bf16[8,128,128]{2,1,0:T(8,128)(2,1)S(1)}, u32[]{:S(2)}, u32[]{:S(2)}) collective-permute-start(bf16[8,128,128]{2,1,0:T(8,128)(2,1)S(1)} %add_convert_fusion.5), channel_id=1, source_target_pairs={{0,16},{8,24},{16,0},{24,8},{1,17},{9,25},{17,1},{25,9},{2,18},{10... | collective-permute-start | bytes 786440 | tf_op jit(solution)/shard_map/ppermute | solution.py:265
  75.7 5.7 %collective-permute-done.19.rest_2_ = bf16[8,128,128]{2,1,0:T(8,128)(2,1)S(1)} collective-permute-done((bf16[8,128,128]{2,1,0:T(8,128)(2,1)S(1)}, bf16[8,128,128]{2,1,0:T(8,128)(2,1)S(1)}, u32[]{:S(2)}, u32[]{:S(2)}) %collective-permute-start.19) | collective-permute-done | bytes 262176 | tf_op jit(solution)/shard_map/ppermute | solution.py:265
  83.5 4.2 %all-to-all-start.2 = ((bf16[32,64,128]{2,1,0:T(8,128)(2,1)}), bf16[32,64,128]{2,1,0:T(8,128)(2,1)}, u32[]{:S(2)}, u32[]{:S(2)}) async-start(bf16[32,64,128]{2,1,0:T(8,128)(2,1)} %pad_maximum_fusion), calls=%async_computation.2 | async-start | bytes 1048576 | tf_op jit(solution)/shard_map/all_to_all | solution.py:369
  87.7 2.1 %add_convert_fusion = bf16[16,128,128]{2,1,0:T(8,128)(2,1)} fusion(bf16[16,128,128]{2,1,0:T(8,128)(2,1)} %collective-permute-done.12, bf16[16,128,128]{2,1,0:T(8,128)(2,1)S(1)} %copy-done.9), kind=kLoop, calls=%fused_computation.4 | loop fusion | flops 1048576 | bytes 1572864 | tf_op jit(solution)/shard_map/convert_element_type | solution.py:329
  89.8 1.7 %collective-permute-start.13 = (bf16[16,128,128]{2,1,0:T(8,128)(2,1)}, bf16[16,128,128]{2,1,0:T(8,128)(2,1)S(1)}, u32[]{:S(2)}, u32[]{:S(2)}) collective-permute-start(bf16[16,128,128]{2,1,0:T(8,128)(2,1)} %add_convert_fusion), channel_id=1, source_target_pairs={{0,1},{2,0},{4,2},{6,4},{7,6},{5,7},{3,5},{1,3},{8,9},{10,8},{12,1... | collective-permute-start | bytes 1572872 | tf_op jit(solution)/shard_map/ppermute | solution.py:243
  91.5 2.0 %add_convert_fusion.2 = bf16[16,128,128]{2,1,0:T(8,128)(2,1)} fusion(bf16[16,128,128]{2,1,0:T(8,128)(2,1)} %collective-permute-done.9, bf16[16,128,128]{2,1,0:T(8,128)(2,1)S(1)} %copy-done.8), kind=kLoop, calls=%fused_computation.6 | loop fusion | flops 1048576 | bytes 1572864 | tf_op jit(solution)/shard_map/convert_element_type | solution.py:329
  94.4 15.7 %collective-permute-done.13.rest_2_ = bf16[16,128,128]{2,1,0:T(8,128)(2,1)S(1)} collective-permute-done((bf16[16,128,128]{2,1,0:T(8,128)(2,1)}, bf16[16,128,128]{2,1,0:T(8,128)(2,1)S(1)}, u32[]{:S(2)}, u32[]{:S(2)}) %collective-permute-start.13) | collective-permute-done | bytes 524320 | tf_op jit(solution)/shard_map/ppermute | solution.py:243
  110.1 2.1 %user_final.1 = (f32[2048,128]{1,0:T(8,128)}, bf16[1024,128]{1,0:T(8,128)(2,1)}) custom-call(f32[2048,128]{1,0:T(8,128)S(1)} %bitcast.20, s32[1024,1]{1,0:T(8,128)S(1)} %reshape_squeeze.8.wanted_ref, bf16[16,128,128]{2,1,0:T(8,128)(2,1)S(1)} %get-tuple-element.35.rest_0_, bf16[16,128,128]{2,1,0:T(8,128)(2,1)S(1)} %collective-permute-done.10.rest_1_, ...), custom_call_target="tpu_custom_call" | custom-call | tf_op jit(solution)/shard_map/user_final/pallas_call | solution.py:170
  112.2 6.5 %all-to-all-start.1 = ((bf16[32,32,128]{2,1,0:T(8,128)(2,1)}), bf16[32,32,128]{2,1,0:T(8,128)(2,1)S(1)}, u32[]{:S(2)}, u32[]{:S(2)}) async-start(bf16[32,32,128]{2,1,0:T(8,128)(2,1)} %bitcast.13), calls=%async_computation.1 | async-start | bytes 524288 | tf_op jit(solution)/shard_map/all_to_all | solution.py:376
  120.1 9.3 %all-to-all-done.1 = bf16[32,32,128]{2,1,0:T(8,128)(2,1)S(1)} async-done(((bf16[32,32,128]{2,1,0:T(8,128)(2,1)}), bf16[32,32,128]{2,1,0:T(8,128)(2,1)S(1)}, u32[]{:S(2)}, u32[]{:S(2)}) %all-to-all-start.1) | async-done | bytes 262176 | tf_op jit(solution)/shard_map/all_to_all | solution.py:376
  129.3 3.5 %bpr_terms.1 = f32[512,1024]{1,0:T(8,128)} custom-call(s32[512,1]{1,0:T(8,128)S(1)} %copy.29.user_slot_ref, s32[512,1]{1,0:T(8,128)S(1)} %copy.30.item_slot_ref, bf16[1024,128]{1,0:T(8,128)(2,1)S(1)} %bitcast.28, bf16[1024,128]{1,0:T(8,128)(2,1)S(1)} %bitcast.30, bf16[1024,128]{1,0:T(8,128)(2,1)S(1)} %bitcast.29), custom_call_target="tpu_custom_call" | custom-call | tf_op jit(solution)/shard_map/bpr_terms/pallas_call | solution.py:201
  (100 shorter events, 22.1 us)
Async XLA Ops:
  2.3 14.9 %collective-permute-start = (bf16[16,128,128]{2,1,0:T(8,128)(2,1)S(1)}, bf16[16,128,128]{2,1,0:T(8,128)(2,1)S(1)}, u32[]{:S(2)}, u32[]{:S(2)}) collective-permute-start(bf16[16,128,128]{2,1,0:T(8,128)(2,1)S(1)} %bitcast.22), channel_id=1, source_target_pairs={{0,2},{2,4},{4,6},{6,7},{7,5},{5,3},{3,1},{1,0},{8,10},{10,12},{12... | collective-permute-start | bytes 1572872 | tf_op jit(solution)/shard_map/ppermute | solution.py:243
  5.4 13.7 %collective-permute-start.2 = (bf16[16,128,128]{2,1,0:T(8,128)(2,1)S(1)}, bf16[16,128,128]{2,1,0:T(8,128)(2,1)S(1)}, u32[]{:S(2)}, u32[]{:S(2)}) collective-permute-start(bf16[16,128,128]{2,1,0:T(8,128)(2,1)S(1)} %bitcast.23), channel_id=1, source_target_pairs={{0,1},{2,0},{4,2},{6,4},{7,6},{5,7},{3,5},{1,3},{8,9},{10,8},{12,1... | collective-permute-start | bytes 1572872 | tf_op jit(solution)/shard_map/ppermute | solution.py:243
  5.5 7.8 %collective-permute-start.4 = (bf16[8,128,128]{2,1,0:T(8,128)(2,1)S(1)}, bf16[8,128,128]{2,1,0:T(8,128)(2,1)S(1)}, u32[]{:S(2)}, u32[]{:S(2)}) collective-permute-start(bf16[8,128,128]{2,1,0:T(8,128)(2,1)S(1)} %bitcast.25), channel_id=1, source_target_pairs={{0,16},{8,24},{16,0},{24,8},{1,17},{9,25},{17,1},{25,9},{2,18},{10... | collective-permute-start | bytes 786440 | tf_op jit(solution)/shard_map/ppermute | solution.py:265
  7.5 12.5 %collective-permute-start.5 = (bf16[8,128,128]{2,1,0:T(8,128)(2,1)S(1)}, bf16[8,128,128]{2,1,0:T(8,128)(2,1)S(1)}, u32[]{:S(2)}, u32[]{:S(2)}) collective-permute-start(bf16[8,128,128]{2,1,0:T(8,128)(2,1)S(1)} %bitcast.26), channel_id=1, source_target_pairs={{0,8},{8,0},{16,24},{24,16},{1,9},{9,1},{17,25},{25,17},{2,10},{10... | collective-permute-start | bytes 786440 | tf_op jit(solution)/shard_map/ppermute | solution.py:265
  13.3 6.7 %collective-permute-start.6 = (bf16[8,128,128]{2,1,0:T(8,128)(2,1)S(1)}, bf16[8,128,128]{2,1,0:T(8,128)(2,1)S(1)}, u32[]{:S(2)}, u32[]{:S(2)}) collective-permute-start(bf16[8,128,128]{2,1,0:T(8,128)(2,1)S(1)} %collective-permute-done.4.rest_1_), channel_id=1, source_target_pairs={{0,8},{8,0},{16,24},{24,16},{1,9},{9,1},{17,25},{25,17},{2,10},{10... | collective-permute-start | bytes 786440 | tf_op jit(solution)/shard_map/ppermute | solution.py:265
  17.3 13.2 %collective-permute-start.1 = (bf16[16,128,128]{2,1,0:T(8,128)(2,1)S(1)}, bf16[16,128,128]{2,1,0:T(8,128)(2,1)}, u32[]{:S(2)}, u32[]{:S(2)}) collective-permute-start(bf16[16,128,128]{2,1,0:T(8,128)(2,1)S(1)} %collective-permute-done.rest_1_), channel_id=1, source_target_pairs={{0,2},{2,4},{4,6},{6,7},{7,5},{5,3},{3,1},{1,0},{8,10},{10,12},{12... | collective-permute-start | bytes 1572872 | tf_op jit(solution)/shard_map/ppermute | solution.py:243
  19.1 12.5 %collective-permute-start.3 = (bf16[16,128,128]{2,1,0:T(8,128)(2,1)S(1)}, bf16[16,128,128]{2,1,0:T(8,128)(2,1)S(1)}, u32[]{:S(2)}, u32[]{:S(2)}) collective-permute-start(bf16[16,128,128]{2,1,0:T(8,128)(2,1)S(1)} %collective-permute-done.2.rest_2_), channel_id=1, source_target_pairs={{0,1},{2,0},{4,2},{6,4},{7,6},{5,7},{3,5},{1,3},{8,9},{10,8},{12,1... | collective-permute-start | bytes 1572872 | tf_op jit(solution)/shard_map/ppermute | solution.py:243
  20.0 40.0 %copy-start.4 = (s32[8,8]{1,0:T(8,128)S(1)}, s32[8,8]{1,0:T(8,128)}, u32[]{:S(2)}) copy-start(s32[8,8]{1,0:T(8,128)} %constant.93.clone.in_ref) | copy-start | bytes 772
  32.4 12.0 %collective-permute-start.15 = (bf16[16,128,128]{2,1,0:T(8,128)(2,1)S(1)}, bf16[16,128,128]{2,1,0:T(8,128)(2,1)S(1)}, u32[]{:S(2)}, u32[]{:S(2)}) collective-permute-start(bf16[16,128,128]{2,1,0:T(8,128)(2,1)S(1)} %collective-permute-done.3.rest_4_), channel_id=1, source_target_pairs={{0,1},{2,0},{4,2},{6,4},{7,6},{5,7},{3,5},{1,3},{8,9},{10,8},{12,1... | collective-permute-start | bytes 1572872 | tf_op jit(solution)/shard_map/ppermute | solution.py:243
  33.7 19.5 %collective-permute-start.7 = (bf16[16,128,128]{2,1,0:T(8,128)(2,1)}, bf16[16,128,128]{2,1,0:T(8,128)(2,1)}, u32[]{:S(2)}, u32[]{:S(2)}) collective-permute-start(bf16[16,128,128]{2,1,0:T(8,128)(2,1)} %get-tuple-element.39), channel_id=1, source_target_pairs={{0,2},{2,4},{4,6},{6,7},{7,5},{5,3},{3,1},{1,0},{8,10},{10,12},{12... | collective-permute-start | bytes 1572872 | tf_op jit(solution)/shard_map/ppermute | solution.py:243
  35.0 22.2 %collective-permute-start.14 = (bf16[16,128,128]{2,1,0:T(8,128)(2,1)}, bf16[16,128,128]{2,1,0:T(8,128)(2,1)S(1)}, u32[]{:S(2)}, u32[]{:S(2)}) collective-permute-start(bf16[16,128,128]{2,1,0:T(8,128)(2,1)} %collective-permute-done.1.rest_3_), channel_id=1, source_target_pairs={{0,2},{2,4},{4,6},{6,7},{7,5},{5,3},{3,1},{1,0},{8,10},{10,12},{12... | collective-permute-start | bytes 1572872 | tf_op jit(solution)/shard_map/ppermute | solution.py:243
  44.4 14.9 %collective-permute-start.16 = (bf16[16,128,128]{2,1,0:T(8,128)(2,1)S(1)}, bf16[16,128,128]{2,1,0:T(8,128)(2,1)S(1)}, u32[]{:S(2)}, u32[]{:S(2)}) collective-permute-start(bf16[16,128,128]{2,1,0:T(8,128)(2,1)S(1)} %collective-permute-done.15.rest_6_), channel_id=1, source_target_pairs={{0,1},{2,0},{4,2},{6,4},{7,6},{5,7},{3,5},{1,3},{8,9},{10,8},{12,1... | collective-permute-start | bytes 1572872 | tf_op jit(solution)/shard_map/ppermute | solution.py:243
  46.8 21.5 %collective-permute-start.11 = (bf16[16,128,128]{2,1,0:T(8,128)(2,1)}, bf16[16,128,128]{2,1,0:T(8,128)(2,1)}, u32[]{:S(2)}, u32[]{:S(2)}) collective-permute-start(bf16[16,128,128]{2,1,0:T(8,128)(2,1)} %get-tuple-element.42), channel_id=1, source_target_pairs={{0,1},{2,0},{4,2},{6,4},{7,6},{5,7},{3,5},{1,3},{8,9},{10,8},{12,1... | collective-permute-start | bytes 1572872 | tf_op jit(solution)/shard_map/ppermute | solution.py:243
  48.2 27.1 %all-to-all-start = ((s32[32,2,32]{2,1,0:T(2,128)}), s32[32,2,32]{2,1,0:T(2,128)S(1)}, u32[]{:S(2)}, u32[]{:S(2)}) async-start(s32[32,2,32]{2,1,0:T(2,128)} %pad_add_fusion), calls=%async_computation | async-start | bytes 65536 | tf_op jit(solution)/shard_map/all_to_all | solution.py:326
  54.5 19.9 %collective-permute-start.8 = (bf16[16,128,128]{2,1,0:T(8,128)(2,1)S(1)}, bf16[16,128,128]{2,1,0:T(8,128)(2,1)S(1)}, u32[]{:S(2)}, u32[]{:S(2)}) collective-permute-start(bf16[16,128,128]{2,1,0:T(8,128)(2,1)S(1)} %add_convert_fusion.4), channel_id=1, source_target_pairs={{0,2},{2,4},{4,6},{6,7},{7,5},{5,3},{3,1},{1,0},{8,10},{10,12},{12... | collective-permute-start | bytes 1572872 | tf_op jit(solution)/shard_map/ppermute | solution.py:243
  68.2 4.5 %collective-permute-start.18 = (bf16[8,128,128]{2,1,0:T(8,128)(2,1)S(1)}, bf16[8,128,128]{2,1,0:T(8,128)(2,1)S(1)}, u32[]{:S(2)}, u32[]{:S(2)}) collective-permute-start(bf16[8,128,128]{2,1,0:T(8,128)(2,1)S(1)} %get-tuple-element.49), channel_id=1, source_target_pairs={{0,8},{8,0},{16,24},{24,16},{1,9},{9,1},{17,25},{25,17},{2,10},{10... | collective-permute-start | bytes 786440 | tf_op jit(solution)/shard_map/ppermute | solution.py:265
  69.6 18.2 %collective-permute-start.12 = (bf16[16,128,128]{2,1,0:T(8,128)(2,1)S(1)}, bf16[16,128,128]{2,1,0:T(8,128)(2,1)}, u32[]{:S(2)}, u32[]{:S(2)}) collective-permute-start(bf16[16,128,128]{2,1,0:T(8,128)(2,1)S(1)} %add_convert_fusion.1), channel_id=1, source_target_pairs={{0,1},{2,0},{4,2},{6,4},{7,6},{5,7},{3,5},{1,3},{8,9},{10,8},{12,1... | collective-permute-start | bytes 1572872 | tf_op jit(solution)/shard_map/ppermute | solution.py:243
  72.6 3.2 %collective-permute-start.17 = (bf16[8,128,128]{2,1,0:T(8,128)(2,1)S(1)}, bf16[8,128,128]{2,1,0:T(8,128)(2,1)S(1)}, u32[]{:S(2)}, u32[]{:S(2)}) collective-permute-start(bf16[8,128,128]{2,1,0:T(8,128)(2,1)S(1)} %get-tuple-element.47), channel_id=1, source_target_pairs={{0,8},{8,0},{16,24},{24,16},{1,9},{9,1},{17,25},{25,17},{2,10},{10... | collective-permute-start | bytes 786440 | tf_op jit(solution)/shard_map/ppermute | solution.py:265
  72.8 8.6 %collective-permute-start.19 = (bf16[8,128,128]{2,1,0:T(8,128)(2,1)S(1)}, bf16[8,128,128]{2,1,0:T(8,128)(2,1)S(1)}, u32[]{:S(2)}, u32[]{:S(2)}) collective-permute-start(bf16[8,128,128]{2,1,0:T(8,128)(2,1)S(1)} %add_convert_fusion.5), channel_id=1, source_target_pairs={{0,16},{8,24},{16,0},{24,8},{1,17},{9,25},{17,1},{25,9},{2,18},{10... | collective-permute-start | bytes 786440 | tf_op jit(solution)/shard_map/ppermute | solution.py:265
  75.3 16.2 %collective-permute-start.9 = (bf16[16,128,128]{2,1,0:T(8,128)(2,1)}, bf16[16,128,128]{2,1,0:T(8,128)(2,1)}, u32[]{:S(2)}, u32[]{:S(2)}) collective-permute-start(bf16[16,128,128]{2,1,0:T(8,128)(2,1)} %add_convert_fusion.3), channel_id=1, source_target_pairs={{0,2},{2,4},{4,6},{6,7},{7,5},{5,3},{3,1},{1,0},{8,10},{10,12},{12... | collective-permute-start | bytes 1572872 | tf_op jit(solution)/shard_map/ppermute | solution.py:243
  83.5 28.8 %all-to-all-start.2 = ((bf16[32,64,128]{2,1,0:T(8,128)(2,1)}), bf16[32,64,128]{2,1,0:T(8,128)(2,1)}, u32[]{:S(2)}, u32[]{:S(2)}) async-start(bf16[32,64,128]{2,1,0:T(8,128)(2,1)} %pad_maximum_fusion), calls=%async_computation.2 | async-start | bytes 1048576 | tf_op jit(solution)/shard_map/all_to_all | solution.py:369
  89.8 20.3 %collective-permute-start.13 = (bf16[16,128,128]{2,1,0:T(8,128)(2,1)}, bf16[16,128,128]{2,1,0:T(8,128)(2,1)S(1)}, u32[]{:S(2)}, u32[]{:S(2)}) collective-permute-start(bf16[16,128,128]{2,1,0:T(8,128)(2,1)} %add_convert_fusion), channel_id=1, source_target_pairs={{0,1},{2,0},{4,2},{6,4},{7,6},{5,7},{3,5},{1,3},{8,9},{10,8},{12,1... | collective-permute-start | bytes 1572872 | tf_op jit(solution)/shard_map/ppermute | solution.py:243
  93.5 16.6 %collective-permute-start.10 = (bf16[16,128,128]{2,1,0:T(8,128)(2,1)}, bf16[16,128,128]{2,1,0:T(8,128)(2,1)S(1)}, u32[]{:S(2)}, u32[]{:S(2)}) collective-permute-start(bf16[16,128,128]{2,1,0:T(8,128)(2,1)} %add_convert_fusion.2), channel_id=1, source_target_pairs={{0,2},{2,4},{4,6},{6,7},{7,5},{5,3},{3,1},{1,0},{8,10},{10,12},{12... | collective-permute-start | bytes 1572872 | tf_op jit(solution)/shard_map/ppermute | solution.py:243
  112.2 17.1 %all-to-all-start.1 = ((bf16[32,32,128]{2,1,0:T(8,128)(2,1)}), bf16[32,32,128]{2,1,0:T(8,128)(2,1)S(1)}, u32[]{:S(2)}, u32[]{:S(2)}) async-start(bf16[32,32,128]{2,1,0:T(8,128)(2,1)} %bitcast.13), calls=%async_computation.1 | async-start | bytes 524288 | tf_op jit(solution)/shard_map/all_to_all | solution.py:376
  (19 other events, 242.5 us)

commit v3 on v2

--- a/solution.py
+++ b/solution.py
@@ -163,7 +163,7 @@
         if transposed:
             prop = prop.T
         final_ref[at, :] = (emb_ref[at, :] + prop) * 0.5
-    picked_rows(wanted_ref, final_ref[...].astype(BF16), rows_ref, 256)
+    picked_rows(wanted_ref, final_ref[...].astype(BF16), rows_ref, 512)
 
 
 def combine(emb, parts, wanted, transposed, name):
@@ -196,7 +196,7 @@
 
 def bpr(user_slot, item_slot, users, items, negatives):
     pairs, embed = user_slot.shape[0], users.shape[1]
-    block = next(b for b in (128, 64, 32, 16, 8, pairs) if pairs % b == 0)
+    block = next(b for b in (256, 128, 64, 32, 16, 8, pairs) if pairs % b == 0)
     whole = lambda array: pl.BlockSpec(array.shape, lambda i: (0, 0))
     return pl.pallas_call(
         bpr_kernel,
@@ -222,6 +222,10 @@
 def requests_of(slot, local, total):
     hits = slot[:, None] == jnp.arange(total, dtype=jnp.int32)[None, :]
     return jnp.sum(jnp.where(hits, local[:, None], 0), axis=0)
+
+
+def after(arrays, *ahead):
+    return lax.optimization_barrier((arrays, ahead))[0]
 
 
 def on_device(user_emb, item_emb, tile_vals, tile_rows, tile_cols, tile_count, pair_users, pair_items, negatives):
@@ -332,7 +336,8 @@
     for s in range(left, 0, -1):
         to_right = around(plus(part[s], to_right), 1)
         if s <= right:
-            to_left = around(plus(part[-s], to_left), -1)
+            mine = part[-s] if to_left is not None else after(part[-s], from_right)
+            to_left = around(plus(mine, to_left), -1)
     user_terms_in = [part[0]] + [more for more in (to_right, to_left) if more is not None]
 
     out_steps = [(j, i) for j in range(row_slow) for i in range(row_fast)]

time: 134 us -> 134 us (level)
  starting transfers between devices: 37.1 us -> 40.8 us
  Pallas kernels: 23.9 us -> 21.6 us
    ppermute x14, starting transfers between devices: 17.6 us -> 24.2 us  [around(): return lax.ppermute(array, 'col', pairs)]
    ppermute x14, waiting for transfers between devices: 32.7 us -> 30.3 us  [around(): return lax.ppermute(array, 'col', pairs)]
    pallas_call x2, Pallas kernels: 17.2 us -> 15.4 us  [terms(): pl.pallas_call(functools.partial(term_kernel, axes=axes, blocks=len(block...]
  transfers between devices with their start and end apart: 23 -> 23, of which waited for: 10 -> 8; matrix products, arithmetic and copies ran while one was open for 10% -> 11% of each run, Pallas kernels for 15% -> 14%
where the time goes in v3:
time: 134 us; the launch traced here: 133 us
  waiting for transfers between devices  52 us (39%)
  starting transfers between devices  40.8 us (30%)
  Pallas kernels  21.6 us (16%)
  other arithmetic  13 us (10%)
  local copies, waits for them, and re-layouts  3.68 us (3%)
  between operations  1.7 us (1%)
    ppermute x14, waiting for transfers between devices, around(): return lax.ppermute(array, 'col', pairs)  30.3 us
    ppermute x14, starting transfers between devices, around(): return lax.ppermute(array, 'col', pairs)  24.2 us
    pallas_call x2, Pallas kernels, terms(): pl.pallas_call(functools.partial(term_kernel, axes=axes, blocks=len(block...  15.4 us
    ppermute x6, waiting for transfers between devices, send_row(): return lax.ppermute(array, 'row', pairs)  12.4 us
    all_to_all x1, waiting for transfers between devices, on_device(): lax.all_to_all(user_rows.reshape(devices, slots, embed), ('row', 'col'),...  9.26 us
    convert_element_type x5, other arithmetic, plus(): (mine.astype(F32) + more.astype(F32)).astype(BF16)  8.19 us
    all_to_all x1, starting transfers between devices, on_device(): lax.all_to_all(user_rows.reshape(devices, slots, embed), ('row', 'col'),...  5.66 us
    all_to_all x1, starting transfers between devices, on_device(): lax.all_to_all(jnp.concatenate([asked_rows, named_rows], axis=1), ('row',...  4.36 us
  transfers between devices with their start and end apart: 23, of which 8 were waited for; matrix products, arithmetic and copies ran while one was open for 11% of the time, Pallas kernels for 14%

profile of v3, /device:TPU:0, one launch (start us, length us, event | category | flops | bytes accessed | tf_op | source)
XLA Modules:
  0.0 132.8 jit_solution(5255934496866143088)
XLA Ops:
  2.3 3.1 %collective-permute-start = (bf16[16,128,128]{2,1,0:T(8,128)(2,1)S(1)}, bf16[16,128,128]{2,1,0:T(8,128)(2,1)S(1)}, u32[]{:S(2)}, u32[]{:S(2)}) collective-permute-start(bf16[16,128,128]{2,1,0:T(8,128)(2,1)S(1)} %bitcast.22), channel_id=1, source_target_pairs={{0,2},{2,4},{4,6},{6,7},{7,5},{5,3},{3,1},{1,0},{8,10},{10,12},{12... | collective-permute-start | bytes 1572872 | tf_op jit(solution)/shard_map/ppermute | solution.py:247
  5.4 2.0 %collective-permute-start.4 = (bf16[8,128,128]{2,1,0:T(8,128)(2,1)S(1)}, bf16[8,128,128]{2,1,0:T(8,128)(2,1)S(1)}, u32[]{:S(2)}, u32[]{:S(2)}) collective-permute-start(bf16[8,128,128]{2,1,0:T(8,128)(2,1)S(1)} %bitcast.25), channel_id=1, source_target_pairs={{0,16},{8,24},{16,0},{24,8},{1,17},{9,25},{17,1},{25,9},{2,18},{10... | collective-permute-start | bytes 786440 | tf_op jit(solution)/shard_map/ppermute | solution.py:269
  7.7 5.5 %collective-permute-done.4.rest_1_ = bf16[8,128,128]{2,1,0:T(8,128)(2,1)S(1)} collective-permute-done((bf16[8,128,128]{2,1,0:T(8,128)(2,1)S(1)}, bf16[8,128,128]{2,1,0:T(8,128)(2,1)S(1)}, u32[]{:S(2)}, u32[]{:S(2)}) %collective-permute-start.4) | collective-permute-done | bytes 262176 | tf_op jit(solution)/shard_map/ppermute | solution.py:269
  13.3 4.0 %collective-permute-done.rest_1_ = bf16[16,128,128]{2,1,0:T(8,128)(2,1)S(1)} collective-permute-done((bf16[16,128,128]{2,1,0:T(8,128)(2,1)S(1)}, bf16[16,128,128]{2,1,0:T(8,128)(2,1)S(1)}, u32[]{:S(2)}, u32[]{:S(2)}) %collective-permute-start) | collective-permute-done | bytes 524320 | tf_op jit(solution)/shard_map/ppermute | solution.py:247
  17.2 1.8 %collective-permute-start.1 = (bf16[16,128,128]{2,1,0:T(8,128)(2,1)S(1)}, bf16[16,128,128]{2,1,0:T(8,128)(2,1)}, u32[]{:S(2)}, u32[]{:S(2)}) collective-permute-start(bf16[16,128,128]{2,1,0:T(8,128)(2,1)S(1)} %collective-permute-done.rest_1_), channel_id=1, source_target_pairs={{0,2},{2,4},{4,6},{6,7},{7,5},{5,3},{3,1},{1,0},{8,10},{10,12},{12... | collective-permute-start | bytes 1572872 | tf_op jit(solution)/shard_map/ppermute | solution.py:247
  20.4 8.1 %user_terms.1 = (bf16[16,128,128]{2,1,0:T(8,128)(2,1)S(1)}, bf16[16,128,128]{2,1,0:T(8,128)(2,1)}, bf16[16,128,128]{2,1,0:T(8,128)(2,1)}, bf16[16,128,128]{2,1,0...) custom-call(s32[1]{0:T(128)} %bitcast.18.count_ref, ...), custom_call_target="tpu_custom_call" | custom-call | flops 2147483648 | bytes 16777216 | tf_op jit(solution)/shard_map/user_terms/pallas_call | solution.py:128
  28.6 5.2 %collective-permute-start.7 = (bf16[16,128,128]{2,1,0:T(8,128)(2,1)}, bf16[16,128,128]{2,1,0:T(8,128)(2,1)S(1)}, u32[]{:S(2)}, u32[]{:S(2)}) collective-permute-start(bf16[16,128,128]{2,1,0:T(8,128)(2,1)} %get-tuple-element.40), channel_id=1, source_target_pairs={{0,2},{2,4},{4,6},{6,7},{7,5},{5,3},{3,1},{1,0},{8,10},{10,12},{12... | collective-permute-start | bytes 1572872 | tf_op jit(solution)/shard_map/ppermute | solution.py:247
  34.1 2.1 %collective-permute-start.16 = (bf16[16,128,128]{2,1,0:T(8,128)(2,1)}, bf16[16,128,128]{2,1,0:T(8,128)(2,1)S(1)}, u32[]{:S(2)}, u32[]{:S(2)}) collective-permute-start(bf16[16,128,128]{2,1,0:T(8,128)(2,1)} %collective-permute-done.1.rest_3_), channel_id=1, source_target_pairs={{0,2},{2,4},{4,6},{6,7},{7,5},{5,3},{3,1},{1,0},{8,10},{10,12},{12... | collective-permute-start | bytes 1572872 | tf_op jit(solution)/shard_map/ppermute | solution.py:247
  36.1 8.6 %collective-permute-done.11.rest_6_ = bf16[16,128,128]{2,1,0:T(8,128)(2,1)S(1)} collective-permute-done((bf16[16,128,128]{2,1,0:T(8,128)(2,1)}, bf16[16,128,128]{2,1,0:T(8,128)(2,1)S(1)}, u32[]{:S(2)}, u32[]{:S(2)}) %collective-permute-start.11) | collective-permute-done | bytes 524320 | tf_op jit(solution)/shard_map/ppermute | solution.py:247
  46.5 2.0 %add_convert_fusion.4 = bf16[16,128,128]{2,1,0:T(8,128)(2,1)} fusion(bf16[16,128,128]{2,1,0:T(8,128)(2,1)S(1)} %collective-permute-done.7, bf16[16,128,128]{2,1,0:T(8,128)(2,1)} %get-tuple-element.39), kind=kLoop, calls=%fused_computation.8 | loop fusion | flops 1048576 | bytes 1572864 | tf_op jit(solution)/shard_map/convert_element_type | solution.py:333
  48.5 2.4 %collective-permute-start.8 = (bf16[16,128,128]{2,1,0:T(8,128)(2,1)}, bf16[16,128,128]{2,1,0:T(8,128)(2,1)}, u32[]{:S(2)}, u32[]{:S(2)}) collective-permute-start(bf16[16,128,128]{2,1,0:T(8,128)(2,1)} %add_convert_fusion.4), channel_id=1, source_target_pairs={{0,2},{2,4},{4,6},{6,7},{7,5},{5,3},{3,1},{1,0},{8,10},{10,12},{12... | collective-permute-start | bytes 1572872 | tf_op jit(solution)/shard_map/ppermute | solution.py:247
  52.6 4.0 %all-to-all-start = ((s32[32,2,32]{2,1,0:T(2,128)}), s32[32,2,32]{2,1,0:T(2,128)S(1)}, u32[]{:S(2)}, u32[]{:S(2)}) async-start(s32[32,2,32]{2,1,0:T(2,128)} %pad_add_fusion), calls=%async_computation | async-start | bytes 65536 | tf_op jit(solution)/shard_map/all_to_all | solution.py:330
  59.3 7.2 %item_terms.1 = (bf16[8,128,128]{2,1,0:T(8,128)(2,1)S(1)}, bf16[8,128,128]{2,1,0:T(8,128)(2,1)S(1)}, bf16[8,128,128]{2,1,0:T(8,128)(2,1)S(1)}, bf16[8,128,128]{2,1,0:T(8,128)(2,1)S(1)}) custom-call(s32[1]{0:T(128)} %bitcast.19.count_ref, s32[512]{0:T(512)S(1)} %bitcast.32, s32[512]{0:T(512)S(1)} %bitcast.34, s32[8,8]{1,0:T(8,128)S(1)} %copy-done.4, ...), custom_call_target="tpu_custom_call" | custom-call | flops 2147483648 | bytes 16777216 | tf_op jit(solution)/shard_map/item_terms/pallas_call | solution.py:128
  67.8 5.0 %collective-permute-start.9 = (bf16[16,128,128]{2,1,0:T(8,128)(2,1)S(1)}, bf16[16,128,128]{2,1,0:T(8,128)(2,1)}, u32[]{:S(2)}, u32[]{:S(2)}) collective-permute-start(bf16[16,128,128]{2,1,0:T(8,128)(2,1)S(1)} %add_convert_fusion.3), channel_id=1, source_target_pairs={{0,2},{2,4},{4,6},{6,7},{7,5},{5,3},{3,1},{1,0},{8,10},{10,12},{12... | collective-permute-start | bytes 1572872 | tf_op jit(solution)/shard_map/ppermute | solution.py:247
  74.8 6.9 %collective-permute-done.19.rest_2_ = bf16[8,128,128]{2,1,0:T(8,128)(2,1)S(1)} collective-permute-done((bf16[8,128,128]{2,1,0:T(8,128)(2,1)S(1)}, bf16[8,128,128]{2,1,0:T(8,128)(2,1)S(1)}, u32[]{:S(2)}, u32[]{:S(2)}) %collective-permute-start.19) | collective-permute-done | bytes 262176 | tf_op jit(solution)/shard_map/ppermute | solution.py:269
  83.9 4.4 %all-to-all-start.2 = ((bf16[32,64,128]{2,1,0:T(8,128)(2,1)}), bf16[32,64,128]{2,1,0:T(8,128)(2,1)}, u32[]{:S(2)}, u32[]{:S(2)}) async-start(bf16[32,64,128]{2,1,0:T(8,128)(2,1)} %pad_maximum_fusion), calls=%async_computation.2 | async-start | bytes 1048576 | tf_op jit(solution)/shard_map/all_to_all | solution.py:374
  88.3 2.1 %add_convert_fusion.2 = bf16[16,128,128]{2,1,0:T(8,128)(2,1)} fusion(bf16[16,128,128]{2,1,0:T(8,128)(2,1)} %collective-permute-done.9, bf16[16,128,128]{2,1,0:T(8,128)(2,1)S(1)} %copy-done.9), kind=kLoop, calls=%fused_computation.6 | loop fusion | flops 1048576 | bytes 1572864 | tf_op jit(solution)/shard_map/convert_element_type | solution.py:333
  92.1 2.0 %add_convert_fusion = bf16[16,128,128]{2,1,0:T(8,128)(2,1)} fusion(bf16[16,128,128]{2,1,0:T(8,128)(2,1)} %collective-permute-done.14, bf16[16,128,128]{2,1,0:T(8,128)(2,1)S(1)} %copy-done.8), kind=kLoop, calls=%fused_computation.4 | loop fusion | flops 1048576 | bytes 1572864 | tf_op jit(solution)/shard_map/convert_element_type | solution.py:333
  94.9 13.7 %collective-permute-done.10.rest_1_ = bf16[16,128,128]{2,1,0:T(8,128)(2,1)S(1)} collective-permute-done((bf16[16,128,128]{2,1,0:T(8,128)(2,1)}, bf16[16,128,128]{2,1,0:T(8,128)(2,1)S(1)}, u32[]{:S(2)}, u32[]{:S(2)}) %collective-permute-start.10) | collective-permute-done | bytes 524320 | tf_op jit(solution)/shard_map/ppermute | solution.py:247
  108.7 2.8 %collective-permute-done.15.rest_2_ = bf16[16,128,128]{2,1,0:T(8,128)(2,1)S(1)} collective-permute-done((bf16[16,128,128]{2,1,0:T(8,128)(2,1)}, bf16[16,128,128]{2,1,0:T(8,128)(2,1)S(1)}, u32[]{:S(2)}, u32[]{:S(2)}) %collective-permute-start.15) | collective-permute-done | bytes 524320 | tf_op jit(solution)/shard_map/ppermute | solution.py:247
  111.5 2.0 %user_final.1 = (f32[2048,128]{1,0:T(8,128)}, bf16[1024,128]{1,0:T(8,128)(2,1)}) custom-call(f32[2048,128]{1,0:T(8,128)S(1)} %bitcast.20, s32[1024,1]{1,0:T(8,128)S(1)} %reshape_squeeze.8.wanted_ref, bf16[16,128,128]{2,1,0:T(8,128)(2,1)S(1)} %get-tuple-element.36.rest_0_, bf16[16,128,128]{2,1,0:T(8,128)(2,1)S(1)} %collective-permute-done.10.rest_1_, ...), custom_call_target="tpu_custom_call" | custom-call | tf_op jit(solution)/shard_map/user_final/pallas_call | solution.py:170
  113.5 5.7 %all-to-all-start.1 = ((bf16[32,32,128]{2,1,0:T(8,128)(2,1)}), bf16[32,32,128]{2,1,0:T(8,128)(2,1)S(1)}, u32[]{:S(2)}, u32[]{:S(2)}) async-start(bf16[32,32,128]{2,1,0:T(8,128)(2,1)} %bitcast.13), calls=%async_computation.1 | async-start | bytes 524288 | tf_op jit(solution)/shard_map/all_to_all | solution.py:381
  120.6 9.3 %all-to-all-done.1 = bf16[32,32,128]{2,1,0:T(8,128)(2,1)S(1)} async-done(((bf16[32,32,128]{2,1,0:T(8,128)(2,1)}), bf16[32,32,128]{2,1,0:T(8,128)(2,1)S(1)}, u32[]{:S(2)}, u32[]{:S(2)}) %all-to-all-start.1) | async-done | bytes 262176 | tf_op jit(solution)/shard_map/all_to_all | solution.py:381
  129.8 3.0 %bpr_terms.1 = f32[512,1024]{1,0:T(8,128)} custom-call(s32[512,1]{1,0:T(8,128)S(1)} %copy.29.user_slot_ref, s32[512,1]{1,0:T(8,128)S(1)} %copy.30.item_slot_ref, bf16[1024,128]{1,0:T(8,128)(2,1)S(1)} %bitcast.28, bf16[1024,128]{1,0:T(8,128)(2,1)S(1)} %bitcast.30, bf16[1024,128]{1,0:T(8,128)(2,1)S(1)} %bitcast.29), custom_call_target="tpu_custom_call" | custom-call | tf_op jit(solution)/shard_map/bpr_terms/pallas_call | solution.py:201
  (96 shorter events, 18.4 us)
Async XLA Ops:
  2.3 14.9 %collective-permute-start = (bf16[16,128,128]{2,1,0:T(8,128)(2,1)S(1)}, bf16[16,128,128]{2,1,0:T(8,128)(2,1)S(1)}, u32[]{:S(2)}, u32[]{:S(2)}) collective-permute-start(bf16[16,128,128]{2,1,0:T(8,128)(2,1)S(1)} %bitcast.22), channel_id=1, source_target_pairs={{0,2},{2,4},{4,6},{6,7},{7,5},{5,3},{3,1},{1,0},{8,10},{10,12},{12... | collective-permute-start | bytes 1572872 | tf_op jit(solution)/shard_map/ppermute | solution.py:247
  5.4 13.7 %collective-permute-start.2 = (bf16[16,128,128]{2,1,0:T(8,128)(2,1)S(1)}, bf16[16,128,128]{2,1,0:T(8,128)(2,1)}, u32[]{:S(2)}, u32[]{:S(2)}) collective-permute-start(bf16[16,128,128]{2,1,0:T(8,128)(2,1)S(1)} %bitcast.23), channel_id=1, source_target_pairs={{0,1},{2,0},{4,2},{6,4},{7,6},{5,7},{3,5},{1,3},{8,9},{10,8},{12,1... | collective-permute-start | bytes 1572872 | tf_op jit(solution)/shard_map/ppermute | solution.py:247
  5.4 7.8 %collective-permute-start.4 = (bf16[8,128,128]{2,1,0:T(8,128)(2,1)S(1)}, bf16[8,128,128]{2,1,0:T(8,128)(2,1)S(1)}, u32[]{:S(2)}, u32[]{:S(2)}) collective-permute-start(bf16[8,128,128]{2,1,0:T(8,128)(2,1)S(1)} %bitcast.25), channel_id=1, source_target_pairs={{0,16},{8,24},{16,0},{24,8},{1,17},{9,25},{17,1},{25,9},{2,18},{10... | collective-permute-start | bytes 786440 | tf_op jit(solution)/shard_map/ppermute | solution.py:269
  7.5 12.8 %collective-permute-start.5 = (bf16[8,128,128]{2,1,0:T(8,128)(2,1)S(1)}, bf16[8,128,128]{2,1,0:T(8,128)(2,1)S(1)}, u32[]{:S(2)}, u32[]{:S(2)}) collective-permute-start(bf16[8,128,128]{2,1,0:T(8,128)(2,1)S(1)} %bitcast.26), channel_id=1, source_target_pairs={{0,8},{8,0},{16,24},{24,16},{1,9},{9,1},{17,25},{25,17},{2,10},{10... | collective-permute-start | bytes 786440 | tf_op jit(solution)/shard_map/ppermute | solution.py:269
  13.3 7.1 %collective-permute-start.6 = (bf16[8,128,128]{2,1,0:T(8,128)(2,1)S(1)}, bf16[8,128,128]{2,1,0:T(8,128)(2,1)S(1)}, u32[]{:S(2)}, u32[]{:S(2)}) collective-permute-start(bf16[8,128,128]{2,1,0:T(8,128)(2,1)S(1)} %collective-permute-done.4.rest_1_), channel_id=1, source_target_pairs={{0,8},{8,0},{16,24},{24,16},{1,9},{9,1},{17,25},{25,17},{2,10},{10... | collective-permute-start | bytes 786440 | tf_op jit(solution)/shard_map/ppermute | solution.py:269
  17.2 16.5 %collective-permute-start.1 = (bf16[16,128,128]{2,1,0:T(8,128)(2,1)S(1)}, bf16[16,128,128]{2,1,0:T(8,128)(2,1)}, u32[]{:S(2)}, u32[]{:S(2)}) collective-permute-start(bf16[16,128,128]{2,1,0:T(8,128)(2,1)S(1)} %collective-permute-done.rest_1_), channel_id=1, source_target_pairs={{0,2},{2,4},{4,6},{6,7},{7,5},{5,3},{3,1},{1,0},{8,10},{10,12},{12... | collective-permute-start | bytes 1572872 | tf_op jit(solution)/shard_map/ppermute | solution.py:247
  19.1 14.7 %collective-permute-start.3 = (bf16[16,128,128]{2,1,0:T(8,128)(2,1)}, bf16[16,128,128]{2,1,0:T(8,128)(2,1)}, u32[]{:S(2)}, u32[]{:S(2)}) collective-permute-start(bf16[16,128,128]{2,1,0:T(8,128)(2,1)} %collective-permute-done.2.rest_2_), channel_id=1, source_target_pairs={{0,1},{2,0},{4,2},{6,4},{7,6},{5,7},{3,5},{1,3},{8,9},{10,8},{12,1... | collective-permute-start | bytes 1572872 | tf_op jit(solution)/shard_map/ppermute | solution.py:247
  20.4 38.9 %copy-start.4 = (s32[8,8]{1,0:T(8,128)S(1)}, s32[8,8]{1,0:T(8,128)}, u32[]{:S(2)}) copy-start(s32[8,8]{1,0:T(8,128)} %constant.93.clone.in_ref) | copy-start | bytes 772
  28.6 17.9 %collective-permute-start.7 = (bf16[16,128,128]{2,1,0:T(8,128)(2,1)}, bf16[16,128,128]{2,1,0:T(8,128)(2,1)S(1)}, u32[]{:S(2)}, u32[]{:S(2)}) collective-permute-start(bf16[16,128,128]{2,1,0:T(8,128)(2,1)} %get-tuple-element.40), channel_id=1, source_target_pairs={{0,2},{2,4},{4,6},{6,7},{7,5},{5,3},{3,1},{1,0},{8,10},{10,12},{12... | collective-permute-start | bytes 1572872 | tf_op jit(solution)/shard_map/ppermute | solution.py:247
  33.8 11.0 %collective-permute-start.11 = (bf16[16,128,128]{2,1,0:T(8,128)(2,1)}, bf16[16,128,128]{2,1,0:T(8,128)(2,1)S(1)}, u32[]{:S(2)}, u32[]{:S(2)}) collective-permute-start(bf16[16,128,128]{2,1,0:T(8,128)(2,1)} %collective-permute-done.3.rest_4_), channel_id=1, source_target_pairs={{0,1},{2,0},{4,2},{6,4},{7,6},{5,7},{3,5},{1,3},{8,9},{10,8},{12,1... | collective-permute-start | bytes 1572872 | tf_op jit(solution)/shard_map/ppermute | solution.py:247
  34.1 24.4 %collective-permute-start.16 = (bf16[16,128,128]{2,1,0:T(8,128)(2,1)}, bf16[16,128,128]{2,1,0:T(8,128)(2,1)S(1)}, u32[]{:S(2)}, u32[]{:S(2)}) collective-permute-start(bf16[16,128,128]{2,1,0:T(8,128)(2,1)} %collective-permute-done.1.rest_3_), channel_id=1, source_target_pairs={{0,2},{2,4},{4,6},{6,7},{7,5},{5,3},{3,1},{1,0},{8,10},{10,12},{12... | collective-permute-start | bytes 1572872 | tf_op jit(solution)/shard_map/ppermute | solution.py:247
  44.7 11.9 %collective-permute-start.12 = (bf16[16,128,128]{2,1,0:T(8,128)(2,1)S(1)}, bf16[16,128,128]{2,1,0:T(8,128)(2,1)S(1)}, u32[]{:S(2)}, u32[]{:S(2)}) collective-permute-start(bf16[16,128,128]{2,1,0:T(8,128)(2,1)S(1)} %collective-permute-done.11.rest_6_), channel_id=1, source_target_pairs={{0,1},{2,0},{4,2},{6,4},{7,6},{5,7},{3,5},{1,3},{8,9},{10,8},{12,1... | collective-permute-start | bytes 1572872 | tf_op jit(solution)/shard_map/ppermute | solution.py:247
  48.5 18.1 %collective-permute-start.8 = (bf16[16,128,128]{2,1,0:T(8,128)(2,1)}, bf16[16,128,128]{2,1,0:T(8,128)(2,1)}, u32[]{:S(2)}, u32[]{:S(2)}) collective-permute-start(bf16[16,128,128]{2,1,0:T(8,128)(2,1)} %add_convert_fusion.4), channel_id=1, source_target_pairs={{0,2},{2,4},{4,6},{6,7},{7,5},{5,3},{3,1},{1,0},{8,10},{10,12},{12... | collective-permute-start | bytes 1572872 | tf_op jit(solution)/shard_map/ppermute | solution.py:247
  52.6 21.8 %all-to-all-start = ((s32[32,2,32]{2,1,0:T(2,128)}), s32[32,2,32]{2,1,0:T(2,128)S(1)}, u32[]{:S(2)}, u32[]{:S(2)}) async-start(s32[32,2,32]{2,1,0:T(2,128)} %pad_add_fusion), calls=%async_computation | async-start | bytes 65536 | tf_op jit(solution)/shard_map/all_to_all | solution.py:330
  56.6 16.9 %collective-permute-start.13 = (bf16[16,128,128]{2,1,0:T(8,128)(2,1)}, bf16[16,128,128]{2,1,0:T(8,128)(2,1)S(1)}, u32[]{:S(2)}, u32[]{:S(2)}) collective-permute-start(bf16[16,128,128]{2,1,0:T(8,128)(2,1)} %get-tuple-element.45), channel_id=1, source_target_pairs={{0,1},{2,0},{4,2},{6,4},{7,6},{5,7},{3,5},{1,3},{8,9},{10,8},{12,1... | collective-permute-start | bytes 1572872 | tf_op jit(solution)/shard_map/ppermute | solution.py:247
  66.5 6.5 %collective-permute-start.18 = (bf16[8,128,128]{2,1,0:T(8,128)(2,1)S(1)}, bf16[8,128,128]{2,1,0:T(8,128)(2,1)S(1)}, u32[]{:S(2)}, u32[]{:S(2)}) collective-permute-start(bf16[8,128,128]{2,1,0:T(8,128)(2,1)S(1)} %get-tuple-element.51), channel_id=1, source_target_pairs={{0,8},{8,0},{16,24},{24,16},{1,9},{9,1},{17,25},{25,17},{2,10},{10... | collective-permute-start | bytes 786440 | tf_op jit(solution)/shard_map/ppermute | solution.py:269
  67.8 20.4 %collective-permute-start.9 = (bf16[16,128,128]{2,1,0:T(8,128)(2,1)S(1)}, bf16[16,128,128]{2,1,0:T(8,128)(2,1)}, u32[]{:S(2)}, u32[]{:S(2)}) collective-permute-start(bf16[16,128,128]{2,1,0:T(8,128)(2,1)S(1)} %add_convert_fusion.3), channel_id=1, source_target_pairs={{0,2},{2,4},{4,6},{6,7},{7,5},{5,3},{3,1},{1,0},{8,10},{10,12},{12... | collective-permute-start | bytes 1572872 | tf_op jit(solution)/shard_map/ppermute | solution.py:247
  72.8 2.0 %collective-permute-start.17 = (bf16[8,128,128]{2,1,0:T(8,128)(2,1)S(1)}, bf16[8,128,128]{2,1,0:T(8,128)(2,1)S(1)}, u32[]{:S(2)}, u32[]{:S(2)}) collective-permute-start(bf16[8,128,128]{2,1,0:T(8,128)(2,1)S(1)} %get-tuple-element.49), channel_id=1, source_target_pairs={{0,8},{8,0},{16,24},{24,16},{1,9},{9,1},{17,25},{25,17},{2,10},{10... | collective-permute-start | bytes 786440 | tf_op jit(solution)/shard_map/ppermute | solution.py:269
  73.1 8.6 %collective-permute-start.19 = (bf16[8,128,128]{2,1,0:T(8,128)(2,1)S(1)}, bf16[8,128,128]{2,1,0:T(8,128)(2,1)S(1)}, u32[]{:S(2)}, u32[]{:S(2)}) collective-permute-start(bf16[8,128,128]{2,1,0:T(8,128)(2,1)S(1)} %add_convert_fusion.5), channel_id=1, source_target_pairs={{0,16},{8,24},{16,0},{24,8},{1,17},{9,25},{17,1},{25,9},{2,18},{10... | collective-permute-start | bytes 786440 | tf_op jit(solution)/shard_map/ppermute | solution.py:269
  74.5 17.6 %collective-permute-start.14 = (bf16[16,128,128]{2,1,0:T(8,128)(2,1)}, bf16[16,128,128]{2,1,0:T(8,128)(2,1)}, u32[]{:S(2)}, u32[]{:S(2)}) collective-permute-start(bf16[16,128,128]{2,1,0:T(8,128)(2,1)} %add_convert_fusion.1), channel_id=1, source_target_pairs={{0,1},{2,0},{4,2},{6,4},{7,6},{5,7},{3,5},{1,3},{8,9},{10,8},{12,1... | collective-permute-start | bytes 1572872 | tf_op jit(solution)/shard_map/ppermute | solution.py:247
  83.9 29.6 %all-to-all-start.2 = ((bf16[32,64,128]{2,1,0:T(8,128)(2,1)}), bf16[32,64,128]{2,1,0:T(8,128)(2,1)}, u32[]{:S(2)}, u32[]{:S(2)}) async-start(bf16[32,64,128]{2,1,0:T(8,128)(2,1)} %pad_maximum_fusion), calls=%async_computation.2 | async-start | bytes 1048576 | tf_op jit(solution)/shard_map/all_to_all | solution.py:374
  90.4 18.3 %collective-permute-start.10 = (bf16[16,128,128]{2,1,0:T(8,128)(2,1)}, bf16[16,128,128]{2,1,0:T(8,128)(2,1)S(1)}, u32[]{:S(2)}, u32[]{:S(2)}) collective-permute-start(bf16[16,128,128]{2,1,0:T(8,128)(2,1)} %add_convert_fusion.2), channel_id=1, source_target_pairs={{0,2},{2,4},{4,6},{6,7},{7,5},{5,3},{3,1},{1,0},{8,10},{10,12},{12... | collective-permute-start | bytes 1572872 | tf_op jit(solution)/shard_map/ppermute | solution.py:247
  94.0 17.4 %collective-permute-start.15 = (bf16[16,128,128]{2,1,0:T(8,128)(2,1)}, bf16[16,128,128]{2,1,0:T(8,128)(2,1)S(1)}, u32[]{:S(2)}, u32[]{:S(2)}) collective-permute-start(bf16[16,128,128]{2,1,0:T(8,128)(2,1)} %add_convert_fusion), channel_id=1, source_target_pairs={{0,1},{2,0},{4,2},{6,4},{7,6},{5,7},{3,5},{1,3},{8,9},{10,8},{12,1... | collective-permute-start | bytes 1572872 | tf_op jit(solution)/shard_map/ppermute | solution.py:247
  113.5 16.3 %all-to-all-start.1 = ((bf16[32,32,128]{2,1,0:T(8,128)(2,1)}), bf16[32,32,128]{2,1,0:T(8,128)(2,1)S(1)}, u32[]{:S(2)}, u32[]{:S(2)}) async-start(bf16[32,32,128]{2,1,0:T(8,128)(2,1)} %bitcast.13), calls=%async_computation.1 | async-start | bytes 524288 | tf_op jit(solution)/shard_map/all_to_all | solution.py:381
  (17 other events, 224.3 us)

commit v4 on v3

--- a/solution.py
+++ b/solution.py
@@ -180,35 +180,56 @@
     )(emb, wanted, *parts)
 
 
-def bpr_kernel(user_slot_ref, item_slot_ref, users_ref, items_ref, negatives_ref, out_ref):
-    def vectors(slot_ref, rows_ref):
-        hot = slot_ref[...] == lax.broadcasted_iota(jnp.int32, (slot_ref.shape[0], rows_ref.shape[0]), 1)
-        return jnp.dot(hot.astype(BF16), rows_ref[...], preferred_element_type=F32)
-
-    users = vectors(user_slot_ref, users_ref)
-    items = vectors(item_slot_ref, items_ref)
-    positive = jnp.sum(users * items, axis=1, keepdims=True)
+def slot_rows(slot_ref, rows_ref):
+    hot = slot_ref[...] == lax.broadcasted_iota(jnp.int32, (slot_ref.shape[0], rows_ref.shape[0]), 1)
+    return jnp.dot(hot.astype(BF16), rows_ref[...], preferred_element_type=F32)
+
+
+def item_vectors_kernel(slot_ref, rows_ref, out_ref):
+    out_ref[...] = slot_rows(slot_ref, rows_ref).astype(BF16)
+
+
+def item_vectors(slot, rows):
+    return pl.pallas_call(
+        item_vectors_kernel,
+        in_specs=[VMEM_WHOLE] * 2,
+        out_specs=VMEM_WHOLE,
+        out_shape=jax.ShapeDtypeStruct((slot.shape[0], rows.shape[1]), BF16),
+        compiler_params=pltpu.CompilerParams(vmem_limit_bytes=32 * 2**20),
+        cost_estimate=pl.CostEstimate(flops=1, bytes_accessed=1, transcendentals=0),
+        name="item_vectors",
+    )(slot, rows)
+
+
+def bpr_kernel(user_slot_ref, users_ref, items_ref, negatives_ref, out_ref):
+    users = slot_rows(user_slot_ref, users_ref)
+    positive = jnp.sum(users * items_ref[...].astype(F32), axis=1, keepdims=True)
     against = lax.dot_general(
         users.astype(BF16), negatives_ref[...], (((1,), (1,)), ((), ())), preferred_element_type=F32
     )
     out_ref[...] = jnp.log1p(jnp.exp(against - positive))
 
 
-def bpr(user_slot, item_slot, users, items, negatives):
+def bpr(user_slot, users, items, negatives):
     pairs, embed = user_slot.shape[0], users.shape[1]
     block = next(b for b in (256, 128, 64, 32, 16, 8, pairs) if pairs % b == 0)
     whole = lambda array: pl.BlockSpec(array.shape, lambda i: (0, 0))
     return pl.pallas_call(
         bpr_kernel,
         grid=(pairs // block,),
-        in_specs=[pl.BlockSpec((block, 1), lambda i: (i, 0))] * 2 + [whole(users), whole(items), whole(negatives)],
+        in_specs=[
+            pl.BlockSpec((block, 1), lambda i: (i, 0)),
+            whole(users),
+            pl.BlockSpec((block, embed), lambda i: (i, 0)),
+            whole(negatives),
+        ],
         out_specs=pl.BlockSpec((block, negatives.shape[0]), lambda i: (i, 0)),
         out_shape=jax.ShapeDtypeStruct((pairs, negatives.shape[0]), F32),
         compiler_params=pltpu.CompilerParams(
             dimension_semantics=("arbitrary",), vmem_limit_bytes=32 * 2**20
         ),
         name="bpr_terms",
-    )(user_slot, item_slot, users, items, negatives)
+    )(user_slot, users, items, negatives)
 
 
 def place_requests(owner, local, slots):
@@ -381,7 +402,8 @@
     user_back = lax.all_to_all(
         user_rows.reshape(devices, slots, embed), ("row", "col"), split_axis=0, concat_axis=0, tiled=True
     ).reshape(devices * slots, embed)
-    bpr_terms = bpr(user_slot[:, None], item_slot[:, None], user_back, item_table_back, negative_rows)
+    items = item_vectors(item_slot[:, None], item_table_back)
+    bpr_terms = bpr(user_slot[:, None], user_back, items, negative_rows)
     return user_final.reshape(user_emb.shape), item_final.reshape(item_emb.shape), bpr_terms
 
 

time: 134 us -> 133 us (level)
  starting transfers between devices: 40.8 us -> 38.1 us
  waiting for transfers between devices: 52 us -> 53.6 us
    ppermute x14, starting transfers between devices: 24.2 us -> 17.6 us  [around(): return lax.ppermute(array, 'col', pairs)]
    ppermute x14, waiting for transfers between devices: 30.3 us -> 35.5 us  [around(): return lax.ppermute(array, 'col', pairs)]
    ppermute x6, waiting for transfers between devices: 12.4 us -> 9.43 us  [send_row(): return lax.ppermute(array, 'row', pairs)]
    ppermute x6, starting transfers between devices: 2.69 us -> 5.64 us  [send_row(): return lax.ppermute(array, 'row', pairs)]
  transfers between devices with their start and end apart: 23 -> 23, of which waited for: 8 -> 9; matrix products, arithmetic and copies ran while one was open for 11% -> 11% of each run, Pallas kernels for 14% -> 15%
where the time goes in v4:
time: 133 us; the launch traced here: 132 us
  waiting for transfers between devices  53.6 us (40%)
  starting transfers between devices  38.1 us (29%)
  Pallas kernels  22 us (17%)
  other arithmetic  13 us (10%)
  local copies, waits for them, and re-layouts  3.8 us (3%)
  between operations  1.65 us (1%)
    ppermute x14, waiting for transfers between devices, around(): return lax.ppermute(array, 'col', pairs)  35.5 us
    ppermute x14, starting transfers between devices, around(): return lax.ppermute(array, 'col', pairs)  17.6 us
    pallas_call x2, Pallas kernels, terms(): pl.pallas_call(functools.partial(term_kernel, axes=axes, blocks=len(block...  15.4 us
    ppermute x6, waiting for transfers between devices, send_row(): return lax.ppermute(array, 'row', pairs)  9.43 us
    all_to_all x1, waiting for transfers between devices, on_device(): lax.all_to_all(user_rows.reshape(devices, slots, embed), ('row', 'col'),...  8.64 us
    convert_element_type x5, other arithmetic, plus(): (mine.astype(F32) + more.astype(F32)).astype(BF16)  8.14 us
    all_to_all x1, starting transfers between devices, on_device(): lax.all_to_all(user_rows.reshape(devices, slots, embed), ('row', 'col'),...  5.66 us
    ppermute x6, starting transfers between devices, send_row(): return lax.ppermute(array, 'row', pairs)  5.64 us
  transfers between devices with their start and end apart: 23, of which 9 were waited for; matrix products, arithmetic and copies ran while one was open for 11% of the time, Pallas kernels for 15%

profile of v4, /device:TPU:0, one launch (start us, length us, event | category | flops | bytes accessed | tf_op | source)
XLA Modules:
  0.0 132.0 jit_solution(6198599270511715652)
XLA Ops:
  2.3 3.1 %collective-permute-start = (bf16[16,128,128]{2,1,0:T(8,128)(2,1)S(1)}, bf16[16,128,128]{2,1,0:T(8,128)(2,1)S(1)}, u32[]{:S(2)}, u32[]{:S(2)}) collective-permute-start(bf16[16,128,128]{2,1,0:T(8,128)(2,1)S(1)} %bitcast.22), channel_id=1, source_target_pairs={{0,2},{2,4},{4,6},{6,7},{7,5},{5,3},{3,1},{1,0},{8,10},{10,12},{12... | collective-permute-start | bytes 1572872 | tf_op jit(solution)/shard_map/ppermute | solution.py:268
  5.4 2.0 %collective-permute-start.4 = (bf16[8,128,128]{2,1,0:T(8,128)(2,1)S(1)}, bf16[8,128,128]{2,1,0:T(8,128)(2,1)S(1)}, u32[]{:S(2)}, u32[]{:S(2)}) collective-permute-start(bf16[8,128,128]{2,1,0:T(8,128)(2,1)S(1)} %bitcast.25), channel_id=1, source_target_pairs={{0,16},{8,24},{16,0},{24,8},{1,17},{9,25},{17,1},{25,9},{2,18},{10... | collective-permute-start | bytes 786440 | tf_op jit(solution)/shard_map/ppermute | solution.py:290
  7.7 5.5 %collective-permute-done.4.rest_1_ = bf16[8,128,128]{2,1,0:T(8,128)(2,1)S(1)} collective-permute-done((bf16[8,128,128]{2,1,0:T(8,128)(2,1)S(1)}, bf16[8,128,128]{2,1,0:T(8,128)(2,1)S(1)}, u32[]{:S(2)}, u32[]{:S(2)}) %collective-permute-start.4) | collective-permute-done | bytes 262176 | tf_op jit(solution)/shard_map/ppermute | solution.py:290
  13.3 4.0 %collective-permute-done.rest_1_ = bf16[16,128,128]{2,1,0:T(8,128)(2,1)S(1)} collective-permute-done((bf16[16,128,128]{2,1,0:T(8,128)(2,1)S(1)}, bf16[16,128,128]{2,1,0:T(8,128)(2,1)S(1)}, u32[]{:S(2)}, u32[]{:S(2)}) %collective-permute-start) | collective-permute-done | bytes 524320 | tf_op jit(solution)/shard_map/ppermute | solution.py:268
  17.2 1.8 %collective-permute-start.1 = (bf16[16,128,128]{2,1,0:T(8,128)(2,1)S(1)}, bf16[16,128,128]{2,1,0:T(8,128)(2,1)}, u32[]{:S(2)}, u32[]{:S(2)}) collective-permute-start(bf16[16,128,128]{2,1,0:T(8,128)(2,1)S(1)} %collective-permute-done.rest_1_), channel_id=1, source_target_pairs={{0,2},{2,4},{4,6},{6,7},{7,5},{5,3},{3,1},{1,0},{8,10},{10,12},{12... | collective-permute-start | bytes 1572872 | tf_op jit(solution)/shard_map/ppermute | solution.py:268
  20.4 8.1 %user_terms.1 = (bf16[16,128,128]{2,1,0:T(8,128)(2,1)S(1)}, bf16[16,128,128]{2,1,0:T(8,128)(2,1)}, bf16[16,128,128]{2,1,0:T(8,128)(2,1)}, bf16[16,128,128]{2,1,0...) custom-call(s32[1]{0:T(128)} %bitcast.18.count_ref, ...), custom_call_target="tpu_custom_call" | custom-call | flops 2147483648 | bytes 16777216 | tf_op jit(solution)/shard_map/user_terms/pallas_call | solution.py:128
  28.6 2.7 %collective-permute-start.7 = (bf16[16,128,128]{2,1,0:T(8,128)(2,1)}, bf16[16,128,128]{2,1,0:T(8,128)(2,1)S(1)}, u32[]{:S(2)}, u32[]{:S(2)}) collective-permute-start(bf16[16,128,128]{2,1,0:T(8,128)(2,1)} %get-tuple-element.40), channel_id=1, source_target_pairs={{0,2},{2,4},{4,6},{6,7},{7,5},{5,3},{3,1},{1,0},{8,10},{10,12},{12... | collective-permute-start | bytes 1572872 | tf_op jit(solution)/shard_map/ppermute | solution.py:268
  34.4 11.6 %collective-permute-done.11.rest_6_ = bf16[16,128,128]{2,1,0:T(8,128)(2,1)S(1)} collective-permute-done((bf16[16,128,128]{2,1,0:T(8,128)(2,1)}, bf16[16,128,128]{2,1,0:T(8,128)(2,1)S(1)}, u32[]{:S(2)}, u32[]{:S(2)}) %collective-permute-start.11) | collective-permute-done | bytes 524320 | tf_op jit(solution)/shard_map/ppermute | solution.py:268
  46.6 2.0 %add_convert_fusion.4 = bf16[16,128,128]{2,1,0:T(8,128)(2,1)} fusion(bf16[16,128,128]{2,1,0:T(8,128)(2,1)S(1)} %collective-permute-done.7, bf16[16,128,128]{2,1,0:T(8,128)(2,1)} %get-tuple-element.39), kind=kLoop, calls=%fused_computation.8 | loop fusion | flops 1048576 | bytes 1572864 | tf_op jit(solution)/shard_map/convert_element_type | solution.py:354
  51.8 4.5 %all-to-all-start = ((s32[32,2,32]{2,1,0:T(2,128)}), s32[32,2,32]{2,1,0:T(2,128)S(1)}, u32[]{:S(2)}, u32[]{:S(2)}) async-start(s32[32,2,32]{2,1,0:T(2,128)} %pad_add_fusion), calls=%async_computation | async-start | bytes 65536 | tf_op jit(solution)/shard_map/all_to_all | solution.py:351
  56.3 2.6 %collective-permute-done.12.rest_7_ = bf16[16,128,128]{2,1,0:T(8,128)(2,1)S(1)} collective-permute-done((bf16[16,128,128]{2,1,0:T(8,128)(2,1)S(1)}, bf16[16,128,128]{2,1,0:T(8,128)(2,1)S(1)}, u32[]{:S(2)}, u32[]{:S(2)}) %collective-permute-start.12) | collective-permute-done | bytes 524320 | tf_op jit(solution)/shard_map/ppermute | solution.py:268
  60.5 7.2 %item_terms.1 = (bf16[8,128,128]{2,1,0:T(8,128)(2,1)S(1)}, bf16[8,128,128]{2,1,0:T(8,128)(2,1)S(1)}, bf16[8,128,128]{2,1,0:T(8,128)(2,1)S(1)}, bf16[8,128,128]{2,1,0:T(8,128)(2,1)S(1)}) custom-call(s32[1]{0:T(128)} %bitcast.19.count_ref, s32[512]{0:T(512)S(1)} %bitcast.32, s32[512]{0:T(512)S(1)} %bitcast.34, s32[8,8]{1,0:T(8,128)S(1)} %copy-done.4, ...), custom_call_target="tpu_custom_call" | custom-call | flops 2147483648 | bytes 16777216 | tf_op jit(solution)/shard_map/item_terms/pallas_call | solution.py:128
  67.8 1.7 %collective-permute-start.18 = (bf16[8,128,128]{2,1,0:T(8,128)(2,1)S(1)}, bf16[8,128,128]{2,1,0:T(8,128)(2,1)S(1)}, u32[]{:S(2)}, u32[]{:S(2)}) collective-permute-start(bf16[8,128,128]{2,1,0:T(8,128)(2,1)S(1)} %get-tuple-element.51), channel_id=1, source_target_pairs={{0,8},{8,0},{16,24},{24,16},{1,9},{9,1},{17,25},{25,17},{2,10},{10... | collective-permute-start | bytes 786440 | tf_op jit(solution)/shard_map/ppermute | solution.py:290
  72.1 1.9 %collective-permute-start.19 = (bf16[8,128,128]{2,1,0:T(8,128)(2,1)S(1)}, bf16[8,128,128]{2,1,0:T(8,128)(2,1)S(1)}, u32[]{:S(2)}, u32[]{:S(2)}) collective-permute-start(bf16[8,128,128]{2,1,0:T(8,128)(2,1)S(1)} %add_convert_fusion.5), channel_id=1, source_target_pairs={{0,16},{8,24},{16,0},{24,8},{1,17},{9,25},{17,1},{25,9},{2,18},{10... | collective-permute-start | bytes 786440 | tf_op jit(solution)/shard_map/ppermute | solution.py:290
  76.9 3.9 %collective-permute-done.19.rest_2_ = bf16[8,128,128]{2,1,0:T(8,128)(2,1)S(1)} collective-permute-done((bf16[8,128,128]{2,1,0:T(8,128)(2,1)S(1)}, bf16[8,128,128]{2,1,0:T(8,128)(2,1)S(1)}, u32[]{:S(2)}, u32[]{:S(2)}) %collective-permute-start.19) | collective-permute-done | bytes 262176 | tf_op jit(solution)/shard_map/ppermute | solution.py:290
  83.0 4.7 %all-to-all-start.2 = ((bf16[32,64,128]{2,1,0:T(8,128)(2,1)}), bf16[32,64,128]{2,1,0:T(8,128)(2,1)}, u32[]{:S(2)}, u32[]{:S(2)}) async-start(bf16[32,64,128]{2,1,0:T(8,128)(2,1)} %pad_maximum_fusion), calls=%async_computation.2 | async-start | bytes 1048576 | tf_op jit(solution)/shard_map/all_to_all | solution.py:395
  87.8 2.1 %add_convert_fusion.2 = bf16[16,128,128]{2,1,0:T(8,128)(2,1)} fusion(bf16[16,128,128]{2,1,0:T(8,128)(2,1)} %collective-permute-done.9, bf16[16,128,128]{2,1,0:T(8,128)(2,1)S(1)} %copy-done.9), kind=kLoop, calls=%fused_computation.6 | loop fusion | flops 1048576 | bytes 1572864 | tf_op jit(solution)/shard_map/convert_element_type | solution.py:354
  91.5 2.0 %add_convert_fusion = bf16[16,128,128]{2,1,0:T(8,128)(2,1)} fusion(bf16[16,128,128]{2,1,0:T(8,128)(2,1)} %collective-permute-done.14, bf16[16,128,128]{2,1,0:T(8,128)(2,1)S(1)} %copy-done.8), kind=kLoop, calls=%fused_computation.4 | loop fusion | flops 1048576 | bytes 1572864 | tf_op jit(solution)/shard_map/convert_element_type | solution.py:354
  94.4 13.7 %collective-permute-done.10.rest_1_ = bf16[16,128,128]{2,1,0:T(8,128)(2,1)S(1)} collective-permute-done((bf16[16,128,128]{2,1,0:T(8,128)(2,1)}, bf16[16,128,128]{2,1,0:T(8,128)(2,1)S(1)}, u32[]{:S(2)}, u32[]{:S(2)}) %collective-permute-start.10) | collective-permute-done | bytes 524320 | tf_op jit(solution)/shard_map/ppermute | solution.py:268
  108.1 2.8 %collective-permute-done.15.rest_2_ = bf16[16,128,128]{2,1,0:T(8,128)(2,1)S(1)} collective-permute-done((bf16[16,128,128]{2,1,0:T(8,128)(2,1)}, bf16[16,128,128]{2,1,0:T(8,128)(2,1)S(1)}, u32[]{:S(2)}, u32[]{:S(2)}) %collective-permute-start.15) | collective-permute-done | bytes 524320 | tf_op jit(solution)/shard_map/ppermute | solution.py:268
  111.0 2.0 %user_final.1 = (f32[2048,128]{1,0:T(8,128)}, bf16[1024,128]{1,0:T(8,128)(2,1)}) custom-call(f32[2048,128]{1,0:T(8,128)S(1)} %bitcast.20, s32[1024,1]{1,0:T(8,128)S(1)} %reshape_squeeze.8.wanted_ref, bf16[16,128,128]{2,1,0:T(8,128)(2,1)S(1)} %get-tuple-element.36.rest_0_, bf16[16,128,128]{2,1,0:T(8,128)(2,1)S(1)} %collective-permute-done.10.rest_1_, ...), custom_call_target="tpu_custom_call" | custom-call | tf_op jit(solution)/shard_map/user_final/pallas_call | solution.py:170
  113.0 5.7 %all-to-all-start.1 = ((bf16[32,32,128]{2,1,0:T(8,128)(2,1)}), bf16[32,32,128]{2,1,0:T(8,128)(2,1)S(1)}, u32[]{:S(2)}, u32[]{:S(2)}) async-start(bf16[32,32,128]{2,1,0:T(8,128)(2,1)} %bitcast.12), calls=%async_computation.1 | async-start | bytes 524288 | tf_op jit(solution)/shard_map/all_to_all | solution.py:402
  120.6 8.6 %all-to-all-done.1 = bf16[32,32,128]{2,1,0:T(8,128)(2,1)S(1)} async-done(((bf16[32,32,128]{2,1,0:T(8,128)(2,1)}), bf16[32,32,128]{2,1,0:T(8,128)(2,1)S(1)}, u32[]{:S(2)}, u32[]{:S(2)}) %all-to-all-start.1) | async-done | bytes 262176 | tf_op jit(solution)/shard_map/all_to_all | solution.py:402
  129.3 2.7 %bpr_terms.1 = f32[512,1024]{1,0:T(8,128)} custom-call(s32[512,1]{1,0:T(8,128)S(1)} %copy.30.user_slot_ref, bf16[1024,128]{1,0:T(8,128)(2,1)S(1)} %bitcast.28, bf16[512,128]{1,0:T(8,128)(2,1)S(1)} %item_vectors.1.items_ref, bf16[1024,128]{1,0:T(8,128)(2,1)S(1)} %bitcast.29), custom_call_target="tpu_custom_call" | custom-call | tf_op jit(solution)/shard_map/bpr_terms/pallas_call | solution.py:217
  (97 shorter events, 23.3 us)
Async XLA Ops:
  2.3 14.9 %collective-permute-start = (bf16[16,128,128]{2,1,0:T(8,128)(2,1)S(1)}, bf16[16,128,128]{2,1,0:T(8,128)(2,1)S(1)}, u32[]{:S(2)}, u32[]{:S(2)}) collective-permute-start(bf16[16,128,128]{2,1,0:T(8,128)(2,1)S(1)} %bitcast.22), channel_id=1, source_target_pairs={{0,2},{2,4},{4,6},{6,7},{7,5},{5,3},{3,1},{1,0},{8,10},{10,12},{12... | collective-permute-start | bytes 1572872 | tf_op jit(solution)/shard_map/ppermute | solution.py:268
  5.4 13.7 %collective-permute-start.2 = (bf16[16,128,128]{2,1,0:T(8,128)(2,1)S(1)}, bf16[16,128,128]{2,1,0:T(8,128)(2,1)}, u32[]{:S(2)}, u32[]{:S(2)}) collective-permute-start(bf16[16,128,128]{2,1,0:T(8,128)(2,1)S(1)} %bitcast.23), channel_id=1, source_target_pairs={{0,1},{2,0},{4,2},{6,4},{7,6},{5,7},{3,5},{1,3},{8,9},{10,8},{12,1... | collective-permute-start | bytes 1572872 | tf_op jit(solution)/shard_map/ppermute | solution.py:268
  5.4 7.8 %collective-permute-start.4 = (bf16[8,128,128]{2,1,0:T(8,128)(2,1)S(1)}, bf16[8,128,128]{2,1,0:T(8,128)(2,1)S(1)}, u32[]{:S(2)}, u32[]{:S(2)}) collective-permute-start(bf16[8,128,128]{2,1,0:T(8,128)(2,1)S(1)} %bitcast.25), channel_id=1, source_target_pairs={{0,16},{8,24},{16,0},{24,8},{1,17},{9,25},{17,1},{25,9},{2,18},{10... | collective-permute-start | bytes 786440 | tf_op jit(solution)/shard_map/ppermute | solution.py:290
  7.5 12.8 %collective-permute-start.5 = (bf16[8,128,128]{2,1,0:T(8,128)(2,1)S(1)}, bf16[8,128,128]{2,1,0:T(8,128)(2,1)S(1)}, u32[]{:S(2)}, u32[]{:S(2)}) collective-permute-start(bf16[8,128,128]{2,1,0:T(8,128)(2,1)S(1)} %bitcast.26), channel_id=1, source_target_pairs={{0,8},{8,0},{16,24},{24,16},{1,9},{9,1},{17,25},{25,17},{2,10},{10... | collective-permute-start | bytes 786440 | tf_op jit(solution)/shard_map/ppermute | solution.py:290
  13.3 7.1 %collective-permute-start.6 = (bf16[8,128,128]{2,1,0:T(8,128)(2,1)S(1)}, bf16[8,128,128]{2,1,0:T(8,128)(2,1)S(1)}, u32[]{:S(2)}, u32[]{:S(2)}) collective-permute-start(bf16[8,128,128]{2,1,0:T(8,128)(2,1)S(1)} %collective-permute-done.4.rest_1_), channel_id=1, source_target_pairs={{0,8},{8,0},{16,24},{24,16},{1,9},{9,1},{17,25},{25,17},{2,10},{10... | collective-permute-start | bytes 786440 | tf_op jit(solution)/shard_map/ppermute | solution.py:290
  17.2 14.0 %collective-permute-start.1 = (bf16[16,128,128]{2,1,0:T(8,128)(2,1)S(1)}, bf16[16,128,128]{2,1,0:T(8,128)(2,1)}, u32[]{:S(2)}, u32[]{:S(2)}) collective-permute-start(bf16[16,128,128]{2,1,0:T(8,128)(2,1)S(1)} %collective-permute-done.rest_1_), channel_id=1, source_target_pairs={{0,2},{2,4},{4,6},{6,7},{7,5},{5,3},{3,1},{1,0},{8,10},{10,12},{12... | collective-permute-start | bytes 1572872 | tf_op jit(solution)/shard_map/ppermute | solution.py:268
  19.1 12.9 %collective-permute-start.3 = (bf16[16,128,128]{2,1,0:T(8,128)(2,1)}, bf16[16,128,128]{2,1,0:T(8,128)(2,1)}, u32[]{:S(2)}, u32[]{:S(2)}) collective-permute-start(bf16[16,128,128]{2,1,0:T(8,128)(2,1)} %collective-permute-done.2.rest_2_), channel_id=1, source_target_pairs={{0,1},{2,0},{4,2},{6,4},{7,6},{5,7},{3,5},{1,3},{8,9},{10,8},{12,1... | collective-permute-start | bytes 1572872 | tf_op jit(solution)/shard_map/ppermute | solution.py:268
  20.4 40.2 %copy-start.4 = (s32[8,8]{1,0:T(8,128)S(1)}, s32[8,8]{1,0:T(8,128)}, u32[]{:S(2)}) copy-start(s32[8,8]{1,0:T(8,128)} %constant.93.clone.in_ref) | copy-start | bytes 772
  28.6 18.0 %collective-permute-start.7 = (bf16[16,128,128]{2,1,0:T(8,128)(2,1)}, bf16[16,128,128]{2,1,0:T(8,128)(2,1)S(1)}, u32[]{:S(2)}, u32[]{:S(2)}) collective-permute-start(bf16[16,128,128]{2,1,0:T(8,128)(2,1)} %get-tuple-element.40), channel_id=1, source_target_pairs={{0,2},{2,4},{4,6},{6,7},{7,5},{5,3},{3,1},{1,0},{8,10},{10,12},{12... | collective-permute-start | bytes 1572872 | tf_op jit(solution)/shard_map/ppermute | solution.py:268
  32.0 14.0 %collective-permute-start.11 = (bf16[16,128,128]{2,1,0:T(8,128)(2,1)}, bf16[16,128,128]{2,1,0:T(8,128)(2,1)S(1)}, u32[]{:S(2)}, u32[]{:S(2)}) collective-permute-start(bf16[16,128,128]{2,1,0:T(8,128)(2,1)} %collective-permute-done.3.rest_4_), channel_id=1, source_target_pairs={{0,1},{2,0},{4,2},{6,4},{7,6},{5,7},{3,5},{1,3},{8,9},{10,8},{12,1... | collective-permute-start | bytes 1572872 | tf_op jit(solution)/shard_map/ppermute | solution.py:268
  32.8 26.8 %collective-permute-start.16 = (bf16[16,128,128]{2,1,0:T(8,128)(2,1)}, bf16[16,128,128]{2,1,0:T(8,128)(2,1)S(1)}, u32[]{:S(2)}, u32[]{:S(2)}) collective-permute-start(bf16[16,128,128]{2,1,0:T(8,128)(2,1)} %collective-permute-done.1.rest_3_), channel_id=1, source_target_pairs={{0,2},{2,4},{4,6},{6,7},{7,5},{5,3},{3,1},{1,0},{8,10},{10,12},{12... | collective-permute-start | bytes 1572872 | tf_op jit(solution)/shard_map/ppermute | solution.py:268
  46.0 12.9 %collective-permute-start.12 = (bf16[16,128,128]{2,1,0:T(8,128)(2,1)S(1)}, bf16[16,128,128]{2,1,0:T(8,128)(2,1)S(1)}, u32[]{:S(2)}, u32[]{:S(2)}) collective-permute-start(bf16[16,128,128]{2,1,0:T(8,128)(2,1)S(1)} %collective-permute-done.11.rest_6_), channel_id=1, source_target_pairs={{0,1},{2,0},{4,2},{6,4},{7,6},{5,7},{3,5},{1,3},{8,9},{10,8},{12,1... | collective-permute-start | bytes 1572872 | tf_op jit(solution)/shard_map/ppermute | solution.py:268
  48.6 20.9 %collective-permute-start.8 = (bf16[16,128,128]{2,1,0:T(8,128)(2,1)}, bf16[16,128,128]{2,1,0:T(8,128)(2,1)}, u32[]{:S(2)}, u32[]{:S(2)}) collective-permute-start(bf16[16,128,128]{2,1,0:T(8,128)(2,1)} %add_convert_fusion.4), channel_id=1, source_target_pairs={{0,2},{2,4},{4,6},{6,7},{7,5},{5,3},{3,1},{1,0},{8,10},{10,12},{12... | collective-permute-start | bytes 1572872 | tf_op jit(solution)/shard_map/ppermute | solution.py:268
  51.8 24.8 %all-to-all-start = ((s32[32,2,32]{2,1,0:T(2,128)}), s32[32,2,32]{2,1,0:T(2,128)S(1)}, u32[]{:S(2)}, u32[]{:S(2)}) async-start(s32[32,2,32]{2,1,0:T(2,128)} %pad_add_fusion), calls=%async_computation | async-start | bytes 65536 | tf_op jit(solution)/shard_map/all_to_all | solution.py:351
  58.9 15.0 %collective-permute-start.13 = (bf16[16,128,128]{2,1,0:T(8,128)(2,1)}, bf16[16,128,128]{2,1,0:T(8,128)(2,1)S(1)}, u32[]{:S(2)}, u32[]{:S(2)}) collective-permute-start(bf16[16,128,128]{2,1,0:T(8,128)(2,1)} %get-tuple-element.45), channel_id=1, source_target_pairs={{0,1},{2,0},{4,2},{6,4},{7,6},{5,7},{3,5},{1,3},{8,9},{10,8},{12,1... | collective-permute-start | bytes 1572872 | tf_op jit(solution)/shard_map/ppermute | solution.py:268
  67.8 4.2 %collective-permute-start.18 = (bf16[8,128,128]{2,1,0:T(8,128)(2,1)S(1)}, bf16[8,128,128]{2,1,0:T(8,128)(2,1)S(1)}, u32[]{:S(2)}, u32[]{:S(2)}) collective-permute-start(bf16[8,128,128]{2,1,0:T(8,128)(2,1)S(1)} %get-tuple-element.51), channel_id=1, source_target_pairs={{0,8},{8,0},{16,24},{24,16},{1,9},{9,1},{17,25},{25,17},{2,10},{10... | collective-permute-start | bytes 786440 | tf_op jit(solution)/shard_map/ppermute | solution.py:290
  70.7 17.1 %collective-permute-start.9 = (bf16[16,128,128]{2,1,0:T(8,128)(2,1)S(1)}, bf16[16,128,128]{2,1,0:T(8,128)(2,1)}, u32[]{:S(2)}, u32[]{:S(2)}) collective-permute-start(bf16[16,128,128]{2,1,0:T(8,128)(2,1)S(1)} %add_convert_fusion.3), channel_id=1, source_target_pairs={{0,2},{2,4},{4,6},{6,7},{7,5},{5,3},{3,1},{1,0},{8,10},{10,12},{12... | collective-permute-start | bytes 1572872 | tf_op jit(solution)/shard_map/ppermute | solution.py:268
  72.0 5.0 %collective-permute-start.17 = (bf16[8,128,128]{2,1,0:T(8,128)(2,1)S(1)}, bf16[8,128,128]{2,1,0:T(8,128)(2,1)S(1)}, u32[]{:S(2)}, u32[]{:S(2)}) collective-permute-start(bf16[8,128,128]{2,1,0:T(8,128)(2,1)S(1)} %get-tuple-element.49), channel_id=1, source_target_pairs={{0,8},{8,0},{16,24},{24,16},{1,9},{9,1},{17,25},{25,17},{2,10},{10... | collective-permute-start | bytes 786440 | tf_op jit(solution)/shard_map/ppermute | solution.py:290
  72.1 8.8 %collective-permute-start.19 = (bf16[8,128,128]{2,1,0:T(8,128)(2,1)S(1)}, bf16[8,128,128]{2,1,0:T(8,128)(2,1)S(1)}, u32[]{:S(2)}, u32[]{:S(2)}) collective-permute-start(bf16[8,128,128]{2,1,0:T(8,128)(2,1)S(1)} %add_convert_fusion.5), channel_id=1, source_target_pairs={{0,16},{8,24},{16,0},{24,8},{1,17},{9,25},{17,1},{25,9},{2,18},{10... | collective-permute-start | bytes 786440 | tf_op jit(solution)/shard_map/ppermute | solution.py:290
  74.9 16.6 %collective-permute-start.14 = (bf16[16,128,128]{2,1,0:T(8,128)(2,1)}, bf16[16,128,128]{2,1,0:T(8,128)(2,1)}, u32[]{:S(2)}, u32[]{:S(2)}) collective-permute-start(bf16[16,128,128]{2,1,0:T(8,128)(2,1)} %add_convert_fusion.1), channel_id=1, source_target_pairs={{0,1},{2,0},{4,2},{6,4},{7,6},{5,7},{3,5},{1,3},{8,9},{10,8},{12,1... | collective-permute-start | bytes 1572872 | tf_op jit(solution)/shard_map/ppermute | solution.py:268
  83.0 29.9 %all-to-all-start.2 = ((bf16[32,64,128]{2,1,0:T(8,128)(2,1)}), bf16[32,64,128]{2,1,0:T(8,128)(2,1)}, u32[]{:S(2)}, u32[]{:S(2)}) async-start(bf16[32,64,128]{2,1,0:T(8,128)(2,1)} %pad_maximum_fusion), calls=%async_computation.2 | async-start | bytes 1048576 | tf_op jit(solution)/shard_map/all_to_all | solution.py:395
  89.8 18.3 %collective-permute-start.10 = (bf16[16,128,128]{2,1,0:T(8,128)(2,1)}, bf16[16,128,128]{2,1,0:T(8,128)(2,1)S(1)}, u32[]{:S(2)}, u32[]{:S(2)}) collective-permute-start(bf16[16,128,128]{2,1,0:T(8,128)(2,1)} %add_convert_fusion.2), channel_id=1, source_target_pairs={{0,2},{2,4},{4,6},{6,7},{7,5},{5,3},{3,1},{1,0},{8,10},{10,12},{12... | collective-permute-start | bytes 1572872 | tf_op jit(solution)/shard_map/ppermute | solution.py:268
  93.5 17.4 %collective-permute-start.15 = (bf16[16,128,128]{2,1,0:T(8,128)(2,1)}, bf16[16,128,128]{2,1,0:T(8,128)(2,1)S(1)}, u32[]{:S(2)}, u32[]{:S(2)}) collective-permute-start(bf16[16,128,128]{2,1,0:T(8,128)(2,1)} %add_convert_fusion), channel_id=1, source_target_pairs={{0,1},{2,0},{4,2},{6,4},{7,6},{5,7},{3,5},{1,3},{8,9},{10,8},{12,1... | collective-permute-start | bytes 1572872 | tf_op jit(solution)/shard_map/ppermute | solution.py:268
  113.0 16.3 %all-to-all-start.1 = ((bf16[32,32,128]{2,1,0:T(8,128)(2,1)}), bf16[32,32,128]{2,1,0:T(8,128)(2,1)S(1)}, u32[]{:S(2)}, u32[]{:S(2)}) async-start(bf16[32,32,128]{2,1,0:T(8,128)(2,1)} %bitcast.12), calls=%async_computation.1 | async-start | bytes 524288 | tf_op jit(solution)/shard_map/all_to_all | solution.py:402
  (17 other events, 224.8 us)
